TPU v7x, 512 devices: a whole 4x4x16 slice. The times are simulated.
512 devices in a mesh: dp: 4 (over x), bank: 128 (over z, y, core).
Axes of the slice: x: 4, y: 4, z: 16, core: 2. Of those that a mesh axis runs over, the one named last changes fastest.
Arguments:
- frames: bfloat16 [8192, 1280], P(('dp', 'bank')), may hold values from -6 to 6
- ln_gain: float32 [1280], replicated, may hold values from 0.5 to 1.5
- w_query: bfloat16 [1280, 256], replicated, may hold values from -0.15625 to 0.15625
- bank_keys: bfloat16 [131072, 256], P('bank'), may hold values from -6 to 6
- bank_values: bfloat16 [131072, 256], P('bank'), may hold values from -6 to 6
- active: int32 [4, 256], replicated, may hold values from 0 to 1023, as said below
- w_out: bfloat16 [256, 1280], replicated, may hold values from -0.375 to 0.375
- ffn_gain: float32 [1280], replicated, may hold values from 0.5 to 1.5
- w_up: bfloat16 [1280, 2560], P(None, 'dp'), may hold values from -0.15625 to 0.15625
- w_down: bfloat16 [2560, 1280], P('dp'), may hold values from -0.125 to 0.125
Outputs:
- layer_out: bfloat16 [8192, 1280], P(('dp', 'bank'))
Inputs may be any that keep to these rules, and one draw needn't show every extreme that they name: `active`: each row lists 256 phrase block ids of one stream; ids may repeat.
All inputs are finite; a program needn't handle non-finite values.
Results may differ from a plain program's by a relative error of at most 0.012.
Values may be sent and summed in bfloat16 or wider, within the bound.
A program may use at most 64 MiB of HBM per device.

v0:
```python
import math

import jax
import jax.numpy as jnp
from jax import lax
from jax.sharding import PartitionSpec as P

BLK = 128


softcap = 30.0


def layer_norm(values, gain_vector):
    wide = values.astype(jnp.float32)
    center = jnp.mean(wide, axis=-1, keepdims=True)
    spread = jnp.mean((wide - center) ** 2, axis=-1, keepdims=True)
    return (wide - center) * lax.rsqrt(spread + 1e-05) * gain_vector


def tile_terms(query_rows, key_tile, value_tile, allow_mask, score_scale):
    raw = lax.dot_general(
        query_rows, key_tile, (((1,), (1,)), ((), ())), preferred_element_type=jnp.float32
    )
    score = softcap * jnp.tanh(raw * score_scale)
    weight = jnp.exp(score)
    weight = jnp.where(allow_mask[None, :], weight, jnp.float32(0.0))
    numerator = jnp.dot(weight.astype(jnp.bfloat16), value_tile, preferred_element_type=jnp.float32)
    return (numerator, jnp.sum(weight, axis=1))


def shard_terms(query_rows, bank_keys, bank_values, block_flags, score_scale):
    row_count = query_rows.shape[0]
    width_bias = query_rows.shape[1]
    allowed = jnp.repeat(block_flags, BLK)
    step_rows = math.gcd(row_count, 512)
    row_blocks = query_rows.reshape(row_count // step_rows, step_rows, width_bias)

    def one_block(block_rows):
        return tile_terms(block_rows, bank_keys, bank_values, allowed, score_scale)

    numerator, totals = lax.map(one_block, row_blocks)
    return (numerator.reshape(row_count, width_bias), totals.reshape(row_count))


def local(frames, ln_gain, w_query, bank_keys, bank_values, active, w_out, ffn_gain, w_up, w_down):
    normed = layer_norm(frames, ln_gain).astype(jnp.bfloat16)
    queries_own = jnp.dot(normed, w_query, preferred_element_type=jnp.float32).astype(jnp.bfloat16)
    queries_all = lax.all_gather(queries_own, "bank", axis=0, tiled=True)
    width_bias = queries_all.shape[1]
    score_scale = 1.0 / (softcap * width_bias**0.5)
    local_blocks = bank_keys.shape[0] // BLK
    chosen = lax.dynamic_index_in_dim(active, lax.axis_index("dp"), 0, keepdims=False)
    first_block = lax.axis_index("bank") * local_blocks
    block_ids = first_block + jnp.arange(local_blocks, dtype=jnp.int32)
    block_flags = jnp.any(block_ids[:, None] == chosen[None, :], axis=1)
    numerator, totals = shard_terms(queries_all, bank_keys, bank_values, block_flags, score_scale)
    numerator, totals = (
        lax.psum_scatter(numerator, "bank", scatter_dimension=0, tiled=True),
        lax.psum_scatter(totals, "bank", scatter_dimension=0, tiled=True),
    )
    context = numerator / totals[:, None]
    context_norm = (
        context * lax.rsqrt(jnp.mean(context * context, axis=1, keepdims=True) + 0.0001)
    ).astype(jnp.bfloat16)
    residual = (
        frames.astype(jnp.float32)
        + jnp.dot(context_norm, w_out, preferred_element_type=jnp.float32)
    ).astype(jnp.bfloat16)
    gathered = lax.all_gather(residual, "dp", axis=0, tiled=True)
    ffn_in = layer_norm(gathered, ffn_gain).astype(jnp.bfloat16)
    pre_act = jnp.dot(ffn_in, w_up, preferred_element_type=jnp.float32)
    hidden = jax.nn.gelu(pre_act, approximate=False).astype(jnp.bfloat16)
    partial_out = jnp.dot(hidden, w_down, preferred_element_type=jnp.float32)
    summed = lax.psum_scatter(
        partial_out.astype(jnp.bfloat16), "dp", scatter_dimension=0, tiled=True
    ).astype(jnp.float32)
    return (residual.astype(jnp.float32) + summed).astype(jnp.bfloat16)


def solution(mesh):
    placed = (
        P(("dp", "bank"), None),
        P(),
        P(),
        P("bank", None),
        P("bank", None),
        P(),
        P(),
        P(),
        P(None, "dp"),
        P("dp", None),
    )
    return jax.shard_map(
        local, mesh=mesh, in_specs=placed, out_specs=P(("dp", "bank"), None), check_vma=False
    )
```

profile of v0, /device:TPU:1, one launch (start us, length us, event | category | flops | bytes accessed | tf_op | source)
XLA Modules:
  0.0 466.6 jit_solution(15526145776370885076)
XLA Ops:
  6.5 1.0 convert_reduce_fusion.1
  7.6 1.0 fusion.34
  8.5 2.0 convolution_convert_fusion.1
  10.7 0.7 constant_dynamic-slice_fusion
  11.4 0.2 compare_reduce_fusion
  11.5 135.6 %all-gather.2.cloned.1.call-done = bf16[2048,256]{1,0:T(8,128)(2,1)} async-done(((bf16[16,256]{1,0:T(8,128)(2,1)}), bf16[2048,256]{1,0:T(8,128)(2,1)}) %all-gather.2.cloned.1.call-update) | async-done | bytes 1048592 | tf_op jit(solution)/shard_map/all_gather | solution.py:49
  147.1 13.8 %while.13 = (s32[]{:T(128)}, f32[4,512,256]{2,1,0:T(8,128)}, f32[4,512]{1,0:T(4,128)S(1)}, bf16[4,512,256]{2,1,0:T(8,128)(2,1)}, bf16[1024,256]{1,0:T(8,128)(2,1...) while((s32[]{:T(128)}, f32[4,512,256]{2,1,0:T(8,128)}, ...), condition=%wide.region_5.6_spmd.clone, body=%wide.region_3.5_spmd.clone.sunk | while | flops 539491840 | bytes 6037653 | solution.py:42
  147.2 2.1 fusion.118
  149.3 1.2 fusion.119
  150.6 2.1 fusion.118
  152.8 1.3 fusion.119
  154.1 2.1 fusion.118
  156.2 1.3 fusion.119
  157.6 2.1 fusion.118
  159.7 1.3 fusion.119
  161.0 1.3 dynamic-slice
  163.0 250.8 %all-reduce = f32[2048]{0:T(1024)S(1)} all-reduce(f32[2048]{0:T(1024)S(1)} %bitcast.41), channel_id=3, replica_groups=mesh['dp'=4,'bank'=128] {'bank'}, use_global_device_ids=true, to_apply=%region_7.8.clone | all-reduce | flops 2048 | bytes 16384
  413.9 0.9 multiply_reduce_fusion
  414.9 1.0 fusion.7
  415.8 9.2 %all_gather.7 = bf16[64,1280]{1,0:T(8,128)(2,1)S(1)} all-gather(bf16[16,1280]{1,0:T(8,128)(2,1)S(1)} %fusion.7), channel_id=1, replica_groups=mesh['dp'=4,'bank'=128] {'dp'}, dimensions={0}, use_global_device_ids=true | all-gather | bytes 204800 | tf_op jit(solution)/shard_map/all_gather | solution.py:70
  425.2 0.2 fusion.10
  425.4 3.2 convolution_convert_fusion
  428.6 30.0 %reduce-scatter.5.cloned.1.call-done = bf16[16,1280]{1,0:T(8,128)(2,1)} async-done(((bf16[64,1280]{1,0:T(8,128)(2,1)}), bf16[16,1280]{1,0:T(8,128)(2,1)}) %reduce-scatter.5.cloned.1.call-update) | async-done | bytes 40976 | tf_op jit(solution)/shard_map/reduce_scatter | solution.py:75
  458.7 1.4 add_convert_fusion
  (42 shorter events, 0.9 us)
Async XLA Ops:
  6.5 418.9 %copy-start = (bf16[640,1280]{1,0:T(8,128)(2,1)S(1)}, bf16[640,1280]{1,0:T(8,128)(2,1)}, u32[]{:S(2)}) copy-start(bf16[640,1280]{1,0:T(8,128)(2,1)} %param.21) | copy-start | bytes 4915204
  6.5 140.6 %all-gather.2.cloned.1.call-start = ((), (), s32[]{:S(2)}) async-start(), calls=%async_computation.2 | async-start | bytes 1056768 | tf_op jit(solution)/shard_map/all_gather | solution.py:49
  10.6 403.4 %reduce-scatter.3.cloned.1.call-start = ((), (), s32[]{:S(2)}) async-start(), calls=%async_computation.3 | async-start | bytes 2113536 | tf_op jit(solution)/shard_map/reduce_scatter | solution.py:59
  147.2 2.1 copy-start.1
  150.6 2.1 copy-start.1
  154.1 2.1 copy-start.1
  157.6 2.1 copy-start.1
  161.0 253.9 %copy-start.2 = (bf16[256,1280]{1,0:T(8,128)(2,1)S(1)}, bf16[256,1280]{1,0:T(8,128)(2,1)}, u32[]{:S(2)}) copy-start(bf16[256,1280]{1,0:T(8,128)(2,1)} %param.18) | copy-start | bytes 1966084
  161.0 253.9 %copy-start.3 = (bf16[16,1280]{1,0:T(8,128)(2,1)S(1)}, bf16[16,1280]{1,0:T(8,128)(2,1)}, u32[]{:S(2)}) copy-start(bf16[16,1280]{1,0:T(8,128)(2,1)} %param.12) | copy-start | bytes 122884
  161.0 264.4 %copy-start.4 = (f32[1280]{0:T(1024)S(1)}, f32[1280]{0:T(1024)}, u32[]{:S(2)}) copy-start(f32[1280]{0:T(1024)} %param.19) | copy-start | bytes 15364
  161.0 297.7 %reduce-scatter.5.cloned.1.call-start = ((), (), s32[]{:S(2)}) async-start(), calls=%async_computation.4 | async-start | bytes 204800 | tf_op jit(solution)/shard_map/reduce_scatter | solution.py:75
Sparse Core Ops, SparseCore 0:
  10.7 136.3 all-gather.1
  161.1 246.1 reduce-scatter.2
  428.7 29.8 reduce-scatter.4
where the time goes:
time: 468 us; the launch traced here: 467 us
  blocking collectives  260 us (56%)
  waiting for transfers between devices  166 us (35%)
  matrix products  19.4 us (4%)
  between operations  13.9 us (3%)
  other arithmetic  4.87 us (1%)
    unnamed x1, blocking collectives  251 us
    all_gather x1, waiting for transfers between devices, local(): queries_all = lax.all_gather(queries_own, 'bank', axis=0, tiled=True)  136 us
    reduce_scatter x1, waiting for transfers between devices, local(): lax.psum_scatter(partial_out.astype(jnp.bfloat16), 'dp', scatter_dimensio...  30 us
  transfers between devices with their start and end apart: 3, of which 2 were waited for; matrix products, arithmetic and copies ran while one was open for 0% of the time, Pallas kernels for 0%

commit v1 on v0

v1 whole, which is shorter than its diff:
```python
import jax
import jax.numpy as jnp
from jax import lax
from jax.experimental import pallas as pl
from jax.experimental.pallas import tpu as pltpu
from jax.sharding import PartitionSpec as P

MESH = pl.DeviceIdType.MESH
F32 = jnp.float32
BF16 = jnp.bfloat16
CAP = 30.0
LOG2E = 1.4426950408889634
NEAR = (0, 1, -1, 2, -2, 3, -3, 4)
NZ, NY, NX = 16, 4, 4
D, FFL, BIAS = 1280, 640, 256
ROWS = 16
PH = 1024
WIDE = BIAS + 128
STEP = 256


def layer_norm(values, gain_row):
    wide = values.astype(F32)
    center = jnp.mean(wide, axis=-1, keepdims=True)
    moved = wide - center
    spread = jnp.mean(moved * moved, axis=-1, keepdims=True)
    return moved * lax.rsqrt(spread + 1e-05) * gain_row


def gelu(v):
    return 0.5 * v * (1.0 + lax.erf(v * 0.7071067811865476))


def kernel(
    frames, ln_gain, w_query, keys, values, active, w_out, ffn_gain, w_up, w_down, out,
    fr, lng, ffg, wq, kb, vb, act, wo, wu, wd,
    qown, qb, pb, po, ry, zs, rz, rs, yo, xr, rc, bias,
    ld, s_kv, r_kv, s_fr, r_fr, s_qx, r_qx, s_q, r_q, s_yf, r_yf, s_ry, r_ry, s_rz, r_rz,
    s_xa, r_xa, s_xr, r_xr, s_rc, r_rc,
):
    x = lax.axis_index("dp")
    b = lax.axis_index("bank")
    c = lax.rem(b, 2)
    y = lax.rem(b // 2, NY)
    z = b // (2 * NY)

    def dev(dx=0, dz=0, dy=0, core=None):
        cz = lax.rem(z + dz + 2 * NZ, NZ)
        cy = lax.rem(y + dy + NY, NY)
        return (lax.rem(x + dx + NX, NX), (cz * NY + cy) * 2 + (c if core is None else core))

    sibling = dev(core=1 - c)

    def send(src, dst, ssem, rsem, to):
        return pltpu.make_async_remote_copy(
            src_ref=src, dst_ref=dst, send_sem=ssem, recv_sem=rsem, device_id=to, device_id_type=MESH
        )

    def arrived(dst, rsem):
        send(dst, dst, rsem, rsem, sibling).wait_recv()

    def far(i):
        return NEAR[i] + (4 if i % 2 else -4) * c

    loads = [
        pltpu.make_async_copy(src, dst, ld.at[n])
        for n, (src, dst) in enumerate(
            (
                (frames, fr.at[pl.ds(ROWS, ROWS)]),
                (ln_gain, lng),
                (w_query, wq),
                (active, act),
                (keys, kb.at[c]),
                (values, vb.at[c]),
                (w_out, wo),
                (ffn_gain, ffg),
                (w_up, wu),
                (w_down, wd),
            )
        )
    ]
    for load in loads:
        load.start()

    barrier = pltpu.get_barrier_semaphore()

    def greet(to):
        pl.semaphore_signal(barrier, inc=1, device_id=to, device_id_type=MESH)

    @pl.when(c == 1)
    def _():
        for dz in (8, 7, -7, 6, -6, 5, -5, 4, -4):
            greet(dev(dz=dz, core=1))
        for dz in NEAR[::-1]:
            greet(dev(dz=-dz, core=0))
        for e in (2, 1, 3):
            greet(dev(dy=e))
            greet(dev(dx=e, core=0))
            greet(dev(dx=e, core=1))

    @pl.when(c == 0)
    def _():
        for dz in NEAR[::-1]:
            greet(dev(dz=dz, core=1))
        for e in (2, 1, 3):
            greet(dev(dy=e))
            greet(dev(dx=e, core=1))

    for n in range(4):
        loads[n].wait()
    normed = layer_norm(fr[ROWS:, :], lng[...]).astype(BF16)
    qown[pl.ds(ROWS, ROWS), :] = jnp.dot(normed, wq[...], preferred_element_type=F32).astype(BF16)

    first = (z * NY + y) * 16
    ids = first + lax.broadcasted_iota(jnp.int32, (16, 256), 0)
    hits = jnp.where(ids == act[pl.ds(x, 1), :], 1.0, 0.0).astype(F32)
    found = jnp.max(hits, axis=1, keepdims=True)
    bias[...] = jnp.broadcast_to(jnp.where(found > 0.5, 0.0, -512.0).astype(F32), (16, 128))

    keys_over = send(keys, kb.at[c], s_kv.at[0], r_kv.at[0], sibling)
    values_over = send(values, vb.at[c], s_kv.at[1], r_kv.at[1], sibling)
    query_over = send(qown.at[pl.ds(ROWS, ROWS)], qown.at[pl.ds(0, ROWS)], s_qx, r_qx, sibling)
    frames_over = send(frames, fr.at[pl.ds(0, ROWS)], s_fr, r_fr, sibling)
    query_out = []
    for core in (1, 0):
        for i in range(7, -1, -1):
            dz = NEAR[i] + (4 if i % 2 else -4) * core
            query_out.append(
                send(
                    qown,
                    qb.at[i // 2, 0, pl.ds((i % 2) * 2 * ROWS, 2 * ROWS)],
                    s_q.at[core * 8 + i],
                    r_q.at[i],
                    dev(dz=-dz, core=core),
                )
            )

    @pl.when(c == 0)
    def _():
        pl.semaphore_wait(barrier, 14)
        query_over.start()

    @pl.when(c == 1)
    def _():
        pl.semaphore_wait(barrier, 26)
        arrived(qown.at[pl.ds(0, ROWS)], r_qx)
        for copy in query_out:
            copy.start()

    keys_over.start()
    values_over.start()

    @pl.when(c == 0)
    def _():
        frames_over.start()

    forward = []
    for k in range(4):
        for j in range(2):
            arrived(qb.at[k, 0, pl.ds(j * 2 * ROWS, 2 * ROWS)], r_q.at[2 * k + j])
        for e in (2, 1, 3):
            copy = send(qb.at[k, 0], qb.at[k, NY - e], s_yf.at[k, e - 1], r_yf.at[k, NY - e - 1], dev(dy=e))
            copy.start()
            forward.append(copy)

    for n in range(4, 6):
        loads[n].wait()
    arrived(kb.at[1 - c], r_kv.at[0])
    arrived(vb.at[1 - c], r_kv.at[1])

    def give_back(k, e):
        return send(pb.at[k, e - 1], ry.at[k, NY - e - 1], s_ry.at[k, e - 1], r_ry.at[k, NY - e - 1], dev(dy=e))

    scale = 1.0 / (CAP * BIAS**0.5)

    def attend(k, carry):
        for e in (1, 3, 2):
            arrived(qb.at[k, e], r_yf.at[k, e - 1])
        q = qb[k].reshape(STEP, BIAS)
        num = jnp.zeros((STEP, BIAS), F32)
        tot = jnp.zeros((STEP, 128), F32)
        for p in range(2 * PH // STEP):
            h, at = (p * STEP) // PH, (p * STEP) % PH
            raw = lax.dot_general(
                q, kb[h, pl.ds(at, STEP), :], (((1,), (1,)), ((), ())), preferred_element_type=F32
            )
            off = jnp.concatenate([bias[pl.ds(2 * p, 1), :], bias[pl.ds(2 * p + 1, 1), :]], axis=1)
            weight = jnp.exp2(jnp.tanh(raw * scale) * (CAP * LOG2E) + off)
            tot = tot + (weight[:, :128] + weight[:, 128:])
            num = num + jnp.dot(weight.astype(BF16), vb[h, pl.ds(at, STEP), :], preferred_element_type=F32)
        part = 4 * ROWS
        po[k, :, :BIAS] = num[:part]
        po[k, :, BIAS:] = tot[:part]
        for e in (1, 2, 3):
            pb[k, e - 1, :, :BIAS] = num[e * part : (e + 1) * part].astype(BF16)
            pb[k, e - 1, :, BIAS:] = tot[e * part : (e + 1) * part].astype(BF16)
        for e in (2, 1, 3):
            give_back(k, e).start()
        return carry

    lax.fori_loop(0, 4, attend, 0)

    sums_out = []
    for k in range(4):
        total = po[k]
        for e in (1, 3, 2):
            arrived(ry.at[k, e - 1], r_ry.at[k, e - 1])
            total = total + ry[k, e - 1].astype(F32)
        zs[k] = total.astype(BF16)
        for j in (1, 0):
            i = 2 * k + j
            copy = send(
                zs.at[k, pl.ds(j * 2 * ROWS, 2 * ROWS)],
                rz.at[c * 8 + i],
                s_rz.at[i],
                r_rz.at[c * 8 + i],
                dev(dz=far(i), core=1),
            )
            copy.start()
            sums_out.append(copy)

    for n in range(6, 10):
        loads[n].wait()

    residual_out = [
        send(rs.at[0], rs.at[NX - e], s_xa.at[e - 1], r_xa.at[NX - e - 1], dev(dx=e)) for e in (2, 1, 3)
    ]
    residual_over = send(rs.at[0, pl.ds(0, ROWS)], rc, s_rc, r_rc, sibling)
    parts_out = [
        send(
            yo.at[e, pl.ds(core * ROWS, ROWS)],
            xr.at[(NX - e) % NX],
            s_xr.at[e * 2 + core],
            r_xr.at[(NX - e) % NX],
            dev(dx=e, core=core),
        )
        for e, core in ((2, 0), (2, 1), (1, 0), (1, 1), (3, 0), (3, 1), (0, 0))
    ]

    @pl.when(c == 1)
    def _():
        arrived(fr.at[pl.ds(0, ROWS)], r_fr)
        total = jnp.zeros((2 * ROWS, WIDE), F32)
        for n in range(16):
            arrived(rz.at[n], r_rz.at[n])
            total = total + rz[n].astype(F32)
        context = total[:, :BIAS] / jnp.sum(total[:, BIAS:], axis=1, keepdims=True)
        power = jnp.mean(context * context, axis=1, keepdims=True)
        context_norm = (context * lax.rsqrt(power + 0.0001)).astype(BF16)
        residual = fr[...].astype(F32) + jnp.dot(context_norm, wo[...], preferred_element_type=F32)
        rs[0] = residual.astype(BF16)
        for copy in residual_out:
            copy.start()
        residual_over.start()
        for e in (1, 3, 2):
            arrived(rs.at[e], r_xa.at[e - 1])
        ffn_in = layer_norm(rs[...].reshape(NX * 2 * ROWS, D), ffg[...]).astype(BF16)
        hidden = gelu(jnp.dot(ffn_in, wu[...], preferred_element_type=F32)).astype(BF16)
        part = jnp.dot(hidden, wd[...], preferred_element_type=F32).astype(BF16)
        yo[...] = part.reshape(NX, 2 * ROWS, D)
        for copy in parts_out:
            copy.start()
        done = rs[0, ROWS:, :].astype(F32) + yo[0, ROWS:, :].astype(F32)
        for e in (1, 3, 2):
            arrived(xr.at[e], r_xr.at[e])
            done = done + xr[e].astype(F32)
        out[...] = done.astype(BF16)

    @pl.when(c == 0)
    def _():
        arrived(rc, r_rc)
        done = rc[...].astype(F32)
        for e in (0, 1, 3, 2):
            arrived(xr.at[e], r_xr.at[e])
            done = done + xr[e].astype(F32)
        out[...] = done.astype(BF16)

    keys_over.wait_send()
    values_over.wait_send()
    for copy in forward + sums_out:
        copy.wait_send()
    for k in range(4):
        for e in (1, 2, 3):
            give_back(k, e).wait_send()

    @pl.when(c == 0)
    def _():
        query_over.wait_send()
        frames_over.wait_send()

    @pl.when(c == 1)
    def _():
        for copy in query_out + residual_out + parts_out:
            copy.wait_send()
        residual_over.wait_send()


def local(*args):
    dma = pltpu.SemaphoreType.DMA
    vm = pltpu.VMEM
    rows = 2 * ROWS
    return pl.pallas_call(
        kernel,
        out_shape=jax.ShapeDtypeStruct((ROWS, D), BF16),
        in_specs=[pl.BlockSpec(memory_space=pl.ANY)] * 10,
        out_specs=pl.BlockSpec(memory_space=pltpu.VMEM),
        scratch_shapes=[
            vm((rows, D), BF16),
            vm((1, D), F32),
            vm((1, D), F32),
            vm((D, BIAS), BF16),
            vm((2, PH, BIAS), BF16),
            vm((2, PH, BIAS), BF16),
            vm((4, 256), jnp.int32),
            vm((BIAS, D), BF16),
            vm((D, FFL), BF16),
            vm((FFL, D), BF16),
            vm((rows, BIAS), BF16),
            vm((4, NY, 2 * rows, BIAS), BF16),
            vm((4, 3, 2 * rows, WIDE), BF16),
            vm((4, 2 * rows, WIDE), F32),
            vm((4, 3, 2 * rows, WIDE), BF16),
            vm((4, 2 * rows, WIDE), BF16),
            vm((16, rows, WIDE), BF16),
            vm((NX, rows, D), BF16),
            vm((NX, rows, D), BF16),
            vm((NX, ROWS, D), BF16),
            vm((ROWS, D), BF16),
            vm((16, 128), F32),
            dma((10,)),
            dma((2,)), dma((2,)),
            dma, dma,
            dma, dma,
            dma((16,)), dma((8,)),
            dma((4, 3)), dma((4, 3)),
            dma((4, 3)), dma((4, 3)),
            dma((8,)), dma((16,)),
            dma((3,)), dma((3,)),
            dma((8,)), dma((4,)),
            dma, dma,
        ],
        compiler_params=pltpu.CompilerParams(
            collective_id=0, has_side_effects=True, vmem_limit_bytes=48 * 2**20
        ),
        name="layer",
    )(*args)


def solution(mesh):
    placed = (
        P(("dp", "bank"), None),
        P(None, None),
        P(),
        P("bank", None),
        P("bank", None),
        P(),
        P(),
        P(None, None),
        P(None, "dp"),
        P("dp", None),
    )
    whole = jax.shard_map(
        local, mesh=mesh, in_specs=placed, out_specs=P(("dp", "bank"), None), check_vma=False
    )

    def step(frames, ln_gain, w_query, bank_keys, bank_values, active, w_out, ffn_gain, w_up, w_down):
        return whole(
            frames, ln_gain[None], w_query, bank_keys, bank_values, active, w_out, ffn_gain[None], w_up, w_down
        )

    return step
```

time: 468 us -> 70.3 us (0.15)
  blocking collectives: 260 us -> 0 us
  waiting for transfers between devices: 166 us -> 0 us
  Pallas kernels: 0 us -> 59.2 us
  matrix products: 19.4 us -> 0 us
  between operations: 13.9 us -> 0.02 us
  local copies, waits for them, and re-layouts: 2.62 us -> 10.6 us
  other arithmetic: 4.87 us -> 0 us
    unnamed x1 -> x0, blocking collectives: 251 us -> none
    all_gather x1 -> x0, waiting for transfers between devices: 136 us -> none  [local(): queries_all = lax.all_gather(queries_own, 'bank', axis=0, tiled=True)]
    pallas_call x0 -> x1, Pallas kernels: none -> 59.2 us  [local(): pl.pallas_call(kernel, out_shape=jax.ShapeDtypeStruct((ROWS, D), BF16), i...]
    reduce_scatter x2 -> x0, waiting for transfers between devices: 30 us -> none  [the longest x1 30 us: local(): lax.psum_scatter(partial_out.astype(jnp.bfloat16), 'dp', scatter_dimensio...]
    dot_general x11 -> x0, matrix products: 19.4 us -> none  [the longest x4 8.28 us: tile_terms(): lax.dot_general(query_rows, key_tile, (((1,), (1,)), ((), ())), preferred...]
    all_gather x1 -> x0, blocking collectives: 9.21 us -> none  [local(): gathered = lax.all_gather(residual, 'dp', axis=0, tiled=True)]
    unnamed x11 -> x17, local copies, waits for them, and re-layouts: 1.42 us -> 9.2 us
  transfers between devices with their start and end apart: 3 -> 0, of which waited for: 2 -> 0; matrix products, arithmetic and copies ran while one was open for 0% -> 0% of each run, Pallas kernels for 0% -> 0%
where the time goes in v1:
time: 70.3 us; the launch traced here: 69.8 us
  Pallas kernels  59.2 us (84%)
  local copies, waits for them, and re-layouts  10.6 us (15%)
    pallas_call x1, Pallas kernels, local(): pl.pallas_call(kernel, out_shape=jax.ShapeDtypeStruct((ROWS, D), BF16), i...  59.2 us
    unnamed x17, local copies, waits for them, and re-layouts  9.2 us

profile of v1, /device:TPU:1, one launch (start us, length us, event | category | flops | bytes accessed | tf_op | source)
XLA Modules:
  0.0 69.8 jit_solution(2662315964103262269)
XLA Ops:
  0.0 0.7 %broadcast_in_dim.6.ln_gain = f32[1,1280]{1,0:T(1,128)S(1)} reshape(f32[1280]{0:T(1024)} %param.11) | data formatting | bytes 10240 | tf_op jit(solution)/broadcast_in_dim | solution.py:368
  0.7 0.7 %broadcast_in_dim.7.ffn_gain = f32[1,1280]{1,0:T(1,128)S(1)} reshape(f32[1280]{0:T(1024)} %param.17) | data formatting | bytes 10240 | tf_op jit(solution)/broadcast_in_dim | solution.py:368
  1.4 0.0 copy-start
  1.4 1.4 %copy-done = bf16[1280,640]{1,0:T(8,128)(2,1)S(1)} copy-done((bf16[1280,640]{1,0:T(8,128)(2,1)S(1)}, bf16[1280,640]{1,0:T(8,128)(2,1)}, u32[]{:S(2)}) %copy-start) | copy-done | bytes 1638424
  2.8 0.0 copy-start.1
  2.8 1.4 %copy-done.1 = bf16[640,1280]{1,0:T(8,128)(2,1)S(1)} copy-done((bf16[640,1280]{1,0:T(8,128)(2,1)S(1)}, bf16[640,1280]{1,0:T(8,128)(2,1)}, u32[]{:S(2)}) %copy-start.1) | copy-done | bytes 1638424
  4.3 0.0 copy-start.2
  4.3 1.1 %copy-done.2 = bf16[1280,256]{1,0:T(8,128)(2,1)S(1)} copy-done((bf16[1280,256]{1,0:T(8,128)(2,1)S(1)}, bf16[1280,256]{1,0:T(8,128)(2,1)}, u32[]{:S(2)}) %copy-start.2) | copy-done | bytes 655384
  5.4 0.0 copy-start.3
  5.4 1.1 %copy-done.3 = bf16[256,1280]{1,0:T(8,128)(2,1)S(1)} copy-done((bf16[256,1280]{1,0:T(8,128)(2,1)S(1)}, bf16[256,1280]{1,0:T(8,128)(2,1)}, u32[]{:S(2)}) %copy-start.3) | copy-done | bytes 655384
  6.4 0.0 copy-start.4
  6.4 1.0 %copy-done.4 = bf16[1024,256]{1,0:T(8,128)(2,1)S(1)} copy-done((bf16[1024,256]{1,0:T(8,128)(2,1)S(1)}, bf16[1024,256]{1,0:T(8,128)(2,1)}, u32[]{:S(2)}) %copy-start.4) | copy-done | bytes 524312
  7.5 0.0 copy-start.5
  7.5 1.0 %copy-done.5 = bf16[1024,256]{1,0:T(8,128)(2,1)S(1)} copy-done((bf16[1024,256]{1,0:T(8,128)(2,1)S(1)}, bf16[1024,256]{1,0:T(8,128)(2,1)}, u32[]{:S(2)}) %copy-start.5) | copy-done | bytes 524312
  8.5 0.0 copy-start.6
  8.5 0.8 %copy-done.6 = bf16[16,1280]{1,0:T(8,128)(2,1)S(1)} copy-done((bf16[16,1280]{1,0:T(8,128)(2,1)S(1)}, bf16[16,1280]{1,0:T(8,128)(2,1)}, u32[]{:S(2)}) %copy-start.6) | copy-done | bytes 40984
  9.3 0.0 copy-start.7
  9.3 0.7 copy-done.7
  10.0 59.2 %layer.1 = bf16[16,1280]{1,0:T(8,128)(2,1)S(1)} custom-call(bf16[16,1280]{1,0:T(8,128)(2,1)S(1)} %copy-done.6, f32[1,1280]{1,0:T(1,128)S(1)} %broadcast_in_dim.6.ln_gain, bf16[1280,256]{1,0:T(8,128)(2,1)S(1)} %copy-done.2, bf16[1024,256]{1,0:T(8,128)(2,1)S(1)} %copy-done.4, bf16[1024,256]{1,0:T(8,128)(2,1)S(1)} %copy-done.5, s32[4,256]{1,0:T(4,128)S(1)} %copy-done.7, ...), custom_call_target="tpu_custom_call" | custom-call | tf_op jit(solution)/shard_map/layer/pallas_call | solution.py:302
  69.2 0.6 copy.12
Async XLA Ops:
  1.4 1.4 %copy-start = (bf16[1280,640]{1,0:T(8,128)(2,1)S(1)}, bf16[1280,640]{1,0:T(8,128)(2,1)}, u32[]{:S(2)}) copy-start(bf16[1280,640]{1,0:T(8,128)(2,1)} %w_up.1) | copy-start | bytes 4915204
  2.8 1.4 %copy-start.1 = (bf16[640,1280]{1,0:T(8,128)(2,1)S(1)}, bf16[640,1280]{1,0:T(8,128)(2,1)}, u32[]{:S(2)}) copy-start(bf16[640,1280]{1,0:T(8,128)(2,1)} %w_down.1) | copy-start | bytes 4915204
  4.3 1.1 %copy-start.2 = (bf16[1280,256]{1,0:T(8,128)(2,1)S(1)}, bf16[1280,256]{1,0:T(8,128)(2,1)}, u32[]{:S(2)}) copy-start(bf16[1280,256]{1,0:T(8,128)(2,1)} %w_query.1) | copy-start | bytes 1966084
  5.4 1.1 %copy-start.3 = (bf16[256,1280]{1,0:T(8,128)(2,1)S(1)}, bf16[256,1280]{1,0:T(8,128)(2,1)}, u32[]{:S(2)}) copy-start(bf16[256,1280]{1,0:T(8,128)(2,1)} %w_out.1) | copy-start | bytes 1966084
  6.4 1.0 %copy-start.4 = (bf16[1024,256]{1,0:T(8,128)(2,1)S(1)}, bf16[1024,256]{1,0:T(8,128)(2,1)}, u32[]{:S(2)}) copy-start(bf16[1024,256]{1,0:T(8,128)(2,1)} %keys.1) | copy-start | bytes 1572868
  7.5 1.0 %copy-start.5 = (bf16[1024,256]{1,0:T(8,128)(2,1)S(1)}, bf16[1024,256]{1,0:T(8,128)(2,1)}, u32[]{:S(2)}) copy-start(bf16[1024,256]{1,0:T(8,128)(2,1)} %values.1) | copy-start | bytes 1572868
  8.5 0.8 %copy-start.6 = (bf16[16,1280]{1,0:T(8,128)(2,1)S(1)}, bf16[16,1280]{1,0:T(8,128)(2,1)}, u32[]{:S(2)}) copy-start(bf16[16,1280]{1,0:T(8,128)(2,1)} %frames.1) | copy-start | bytes 122884
  9.3 0.7 copy-start.7

commit v2 on v1

--- a/solution.py
+++ b/solution.py
@@ -19,12 +19,12 @@
 STEP = 256
 
 
-def layer_norm(values, gain_row):
+def layer_norm(values, gain):
     wide = values.astype(F32)
     center = jnp.mean(wide, axis=-1, keepdims=True)
     moved = wide - center
     spread = jnp.mean(moved * moved, axis=-1, keepdims=True)
-    return moved * lax.rsqrt(spread + 1e-05) * gain_row
+    return moved * lax.rsqrt(spread + 1e-05) * gain[None, :]
 
 
 def gelu(v):
@@ -34,8 +34,8 @@
 def kernel(
     frames, ln_gain, w_query, keys, values, active, w_out, ffn_gain, w_up, w_down, out,
     fr, lng, ffg, wq, kb, vb, act, wo, wu, wd,
-    qown, qb, pb, po, ry, zs, rz, rs, yo, xr, rc, bias,
-    ld, s_kv, r_kv, s_fr, r_fr, s_qx, r_qx, s_q, r_q, s_yf, r_yf, s_ry, r_ry, s_rz, r_rz,
+    qown, qb, pb, po, ry, zs, rz, rs, yo, xr, rc, bias, wb,
+    ld, s_kv, r_kv, s_fr, r_fr, s_qx, r_qx, s_q, r_q, s_fw, s_yf, r_yf, s_ry, r_ry, s_rz, r_rz,
     s_xa, r_xa, s_xr, r_xr, s_rc, r_rc,
 ):
     x = lax.axis_index("dp")
@@ -82,6 +82,22 @@
     for load in loads:
         load.start()
 
+    sent, sent0, sent1 = [], [], []
+
+    def finish():
+        for copy in sent:
+            copy.wait_send()
+
+        @pl.when(c == 0)
+        def _():
+            for copy in sent0:
+                copy.wait_send()
+
+        @pl.when(c == 1)
+        def _():
+            for copy in sent1:
+                copy.wait_send()
+
     barrier = pltpu.get_barrier_semaphore()
 
     def greet(to):
@@ -89,9 +105,9 @@
 
     @pl.when(c == 1)
     def _():
-        for dz in (8, 7, -7, 6, -6, 5, -5, 4, -4):
+        for dz in (4, -4, 3, -3, 2, -2, 1, -1):
             greet(dev(dz=dz, core=1))
-        for dz in NEAR[::-1]:
+        for dz in NEAR[::-1] + (-4,):
             greet(dev(dz=-dz, core=0))
         for e in (2, 1, 3):
             greet(dev(dy=e))
@@ -100,7 +116,7 @@
 
     @pl.when(c == 0)
     def _():
-        for dz in NEAR[::-1]:
+        for dz in NEAR[::-1] + (-4,):
             greet(dev(dz=dz, core=1))
         for e in (2, 1, 3):
             greet(dev(dy=e))
@@ -121,23 +137,23 @@
     values_over = send(values, vb.at[c], s_kv.at[1], r_kv.at[1], sibling)
     query_over = send(qown.at[pl.ds(ROWS, ROWS)], qown.at[pl.ds(0, ROWS)], s_qx, r_qx, sibling)
     frames_over = send(frames, fr.at[pl.ds(0, ROWS)], s_fr, r_fr, sibling)
-    query_out = []
-    for core in (1, 0):
-        for i in range(7, -1, -1):
-            dz = NEAR[i] + (4 if i % 2 else -4) * core
-            query_out.append(
-                send(
-                    qown,
-                    qb.at[i // 2, 0, pl.ds((i % 2) * 2 * ROWS, 2 * ROWS)],
-                    s_q.at[core * 8 + i],
-                    r_q.at[i],
-                    dev(dz=-dz, core=core),
-                )
-            )
-
-    @pl.when(c == 0)
-    def _():
-        pl.semaphore_wait(barrier, 14)
+    def slot(i):
+        return qb.at[i // 2, 0, pl.ds((i % 2) * 2 * ROWS, 2 * ROWS)]
+
+    query_out = [send(qown, slot(0), s_q.at[8], r_q.at[0], dev(dz=4, core=1))] + [
+        send(qown, slot(i), s_q.at[i], r_q.at[i], dev(dz=-NEAR[i], core=0)) for i in range(7, -1, -1)
+    ]
+    relay0 = [send(slot(7), slot(i), s_fw.at[i // 2], r_q.at[i], dev(dz=-(i // 2 + 1), core=1)) for i in (7, 5, 3, 1)]
+    relay1 = [send(slot(0), slot(i), s_fw.at[i // 2], r_q.at[i], dev(dz=i // 2, core=1)) for i in (6, 4, 2)]
+
+    sent0 += [query_over, frames_over]
+    sent0 += relay0
+    sent1 += query_out + relay1
+    sent += [keys_over, values_over]
+
+    @pl.when(c == 0)
+    def _():
+        pl.semaphore_wait(barrier, 15)
         query_over.start()
 
     @pl.when(c == 1)
@@ -154,14 +170,33 @@
     def _():
         frames_over.start()
 
-    forward = []
+    @pl.when(c == 0)
+    def _():
+        arrived(slot(7), r_q.at[7])
+        for copy in relay0:
+            copy.start()
+        arrived(slot(0), r_q.at[0])
+
+    @pl.when(c == 1)
+    def _():
+        arrived(slot(0), r_q.at[0])
+        for copy in relay1:
+            copy.start()
+
     for k in range(4):
-        for j in range(2):
-            arrived(qb.at[k, 0, pl.ds(j * 2 * ROWS, 2 * ROWS)], r_q.at[2 * k + j])
+        for i in (2 * k, 2 * k + 1):
+            if 0 < i < 7:
+                arrived(slot(i), r_q.at[i])
+        if k == 3:
+
+            @pl.when(c == 1)
+            def _():
+                arrived(slot(7), r_q.at[7])
+
         for e in (2, 1, 3):
             copy = send(qb.at[k, 0], qb.at[k, NY - e], s_yf.at[k, e - 1], r_yf.at[k, NY - e - 1], dev(dy=e))
             copy.start()
-            forward.append(copy)
+            sent.append(copy)
 
     for n in range(4, 6):
         loads[n].wait()
@@ -177,7 +212,6 @@
         for e in (1, 3, 2):
             arrived(qb.at[k, e], r_yf.at[k, e - 1])
         q = qb[k].reshape(STEP, BIAS)
-        num = jnp.zeros((STEP, BIAS), F32)
         tot = jnp.zeros((STEP, 128), F32)
         for p in range(2 * PH // STEP):
             h, at = (p * STEP) // PH, (p * STEP) % PH
@@ -187,7 +221,8 @@
             off = jnp.concatenate([bias[pl.ds(2 * p, 1), :], bias[pl.ds(2 * p + 1, 1), :]], axis=1)
             weight = jnp.exp2(jnp.tanh(raw * scale) * (CAP * LOG2E) + off)
             tot = tot + (weight[:, :128] + weight[:, 128:])
-            num = num + jnp.dot(weight.astype(BF16), vb[h, pl.ds(at, STEP), :], preferred_element_type=F32)
+            wb[:, p * STEP : (p + 1) * STEP] = weight.astype(BF16)
+        num = jnp.dot(wb[...], vb[...].reshape(2 * PH, BIAS), preferred_element_type=F32)
         part = 4 * ROWS
         po[k, :, :BIAS] = num[:part]
         po[k, :, BIAS:] = tot[:part]
@@ -199,8 +234,8 @@
         return carry
 
     lax.fori_loop(0, 4, attend, 0)
-
-    sums_out = []
+    sent += [give_back(k, e) for k in range(4) for e in (1, 2, 3)]
+
     for k in range(4):
         total = po[k]
         for e in (1, 3, 2):
@@ -217,7 +252,7 @@
                 dev(dz=far(i), core=1),
             )
             copy.start()
-            sums_out.append(copy)
+            sent.append(copy)
 
     for n in range(6, 10):
         loads[n].wait()
@@ -237,6 +272,8 @@
         for e, core in ((2, 0), (2, 1), (1, 0), (1, 1), (3, 0), (3, 1), (0, 0))
     ]
 
+    sent1 += residual_out + parts_out + [residual_over]
+
     @pl.when(c == 1)
     def _():
         arrived(fr.at[pl.ds(0, ROWS)], r_fr)
@@ -275,24 +312,7 @@
             done = done + xr[e].astype(F32)
         out[...] = done.astype(BF16)
 
-    keys_over.wait_send()
-    values_over.wait_send()
-    for copy in forward + sums_out:
-        copy.wait_send()
-    for k in range(4):
-        for e in (1, 2, 3):
-            give_back(k, e).wait_send()
-
-    @pl.when(c == 0)
-    def _():
-        query_over.wait_send()
-        frames_over.wait_send()
-
-    @pl.when(c == 1)
-    def _():
-        for copy in query_out + residual_out + parts_out:
-            copy.wait_send()
-        residual_over.wait_send()
+    finish()
 
 
 def local(*args):
@@ -302,12 +322,12 @@
     return pl.pallas_call(
         kernel,
         out_shape=jax.ShapeDtypeStruct((ROWS, D), BF16),
-        in_specs=[pl.BlockSpec(memory_space=pl.ANY)] * 10,
+        in_specs=[pl.BlockSpec(memory_space=pltpu.HBM)] * 10,
         out_specs=pl.BlockSpec(memory_space=pltpu.VMEM),
         scratch_shapes=[
             vm((rows, D), BF16),
-            vm((1, D), F32),
-            vm((1, D), F32),
+            vm((D,), F32),
+            vm((D,), F32),
             vm((D, BIAS), BF16),
             vm((2, PH, BIAS), BF16),
             vm((2, PH, BIAS), BF16),
@@ -327,11 +347,12 @@
             vm((NX, ROWS, D), BF16),
             vm((ROWS, D), BF16),
             vm((16, 128), F32),
+            vm((STEP, 2 * PH), BF16),
             dma((10,)),
             dma((2,)), dma((2,)),
             dma, dma,
             dma, dma,
-            dma((16,)), dma((8,)),
+            dma((9,)), dma((8,)), dma((4,)),
             dma((4, 3)), dma((4, 3)),
             dma((4, 3)), dma((4, 3)),
             dma((8,)), dma((16,)),
@@ -340,7 +361,7 @@
             dma, dma,
         ],
         compiler_params=pltpu.CompilerParams(
-            collective_id=0, has_side_effects=True, vmem_limit_bytes=48 * 2**20
+            collective_id=0, has_side_effects=True, vmem_limit_bytes=56 * 2**20
         ),
         name="layer",
     )(*args)
@@ -349,23 +370,16 @@
 def solution(mesh):
     placed = (
         P(("dp", "bank"), None),
-        P(None, None),
+        P(),
         P(),
         P("bank", None),
         P("bank", None),
         P(),
         P(),
-        P(None, None),
+        P(),
         P(None, "dp"),
         P("dp", None),
     )
-    whole = jax.shard_map(
+    return jax.shard_map(
         local, mesh=mesh, in_specs=placed, out_specs=P(("dp", "bank"), None), check_vma=False
     )
-
-    def step(frames, ln_gain, w_query, bank_keys, bank_values, active, w_out, ffn_gain, w_up, w_down):
-        return whole(
-            frames, ln_gain[None], w_query, bank_keys, bank_values, active, w_out, ffn_gain[None], w_up, w_down
-        )
-
-    return step

time: 70.3 us -> 59.8 us (0.85)
  local copies, waits for them, and re-layouts: 10.6 us -> 1.4 us
  Pallas kernels: 59.2 us -> 58.2 us
    unnamed x17 -> x1, local copies, waits for them, and re-layouts: 9.2 us -> 1.4 us
    broadcast_in_dim x2 -> x0, local copies, waits for them, and re-layouts: 1.4 us -> none  [the longest x1 0.7 us: step(): ln_gain[None]]
    pallas_call x1, Pallas kernels: 59.2 us -> 58.2 us  [local(): pl.pallas_call(kernel, out_shape=jax.ShapeDtypeStruct((ROWS, D), BF16), i...]
where the time goes in v2:
time: 59.8 us; the launch traced here: 59.6 us
  Pallas kernels  58.2 us (97%)
  local copies, waits for them, and re-layouts  1.4 us (2%)
    pallas_call x1, Pallas kernels, local(): pl.pallas_call(kernel, out_shape=jax.ShapeDtypeStruct((ROWS, D), BF16), i...  58.2 us
    unnamed x1, local copies, waits for them, and re-layouts  1.4 us

profile of v2, /device:TPU:1, one launch (start us, length us, event | category | flops | bytes accessed | tf_op | source)
XLA Modules:
  0.0 59.6 jit_solution(5225453467709406579)
XLA Ops:
  0.0 58.2 %layer.1 = bf16[16,1280]{1,0:T(8,128)(2,1)} custom-call(bf16[16,1280]{1,0:T(8,128)(2,1)} %frames.1, f32[1280]{0:T(1024)} %ln_gain.1, bf16[1280,256]{1,0:T(8,128)(2,1)} %w_query.1, bf16[1024,256]{1,0:T(8,128)(2,1)} %keys.1, bf16[1024,256]{1,0:T(8,128)(2,1)} %values.1, s32[4,256]{1,0:T(4,128)} %active.1, bf16[256,1280]{1,0:T(8,128)(2,1)} %w_out.1, ...), custom_call_target="tpu_custom_call" | custom-call | tf_op jit(solution)/shard_map/layer/pallas_call | solution.py:322
  58.2 1.4 %copy.12 = bf16[16,1280]{1,0:T(8,128)(2,1)} copy(bf16[16,1280]{1,0:T(8,128)(2,1)} %layer.1) | data formatting | bytes 81920

commit v3 on v2

--- a/solution.py
+++ b/solution.py
@@ -10,7 +10,7 @@
 BF16 = jnp.bfloat16
 CAP = 30.0
 LOG2E = 1.4426950408889634
-NEAR = (0, 1, -1, 2, -2, 3, -3, 4)
+NEAR = (0, -1, -2, -3, 1, 2, 3, 4)
 NZ, NY, NX = 16, 4, 4
 D, FFL, BIAS = 1280, 640, 256
 ROWS = 16
@@ -34,15 +34,16 @@
 def kernel(
     frames, ln_gain, w_query, keys, values, active, w_out, ffn_gain, w_up, w_down, out,
     fr, lng, ffg, wq, kb, vb, act, wo, wu, wd,
-    qown, qb, pb, po, ry, zs, rz, rs, yo, xr, rc, bias, wb,
+    qown, qb, pb, po, ry, zs, rz, cx, rs, yo, xr, rc, bias, wb,
     ld, s_kv, r_kv, s_fr, r_fr, s_qx, r_qx, s_q, r_q, s_fw, s_yf, r_yf, s_ry, r_ry, s_rz, r_rz,
-    s_xa, r_xa, s_xr, r_xr, s_rc, r_rc,
+    s_xf, r_xf, s_xa, r_xa, s_xr, r_xr, s_rc, r_rc,
 ):
     x = lax.axis_index("dp")
     b = lax.axis_index("bank")
     c = lax.rem(b, 2)
     y = lax.rem(b // 2, NY)
     z = b // (2 * NY)
+    upper = z // (NZ // 2)
 
     def dev(dx=0, dz=0, dy=0, core=None):
         cz = lax.rem(z + dz + 2 * NZ, NZ)
@@ -59,14 +60,11 @@
     def arrived(dst, rsem):
         send(dst, dst, rsem, rsem, sibling).wait_recv()
 
-    def far(i):
-        return NEAR[i] + (4 if i % 2 else -4) * c
-
     loads = [
         pltpu.make_async_copy(src, dst, ld.at[n])
         for n, (src, dst) in enumerate(
             (
-                (frames, fr.at[pl.ds(ROWS, ROWS)]),
+                (frames, fr.at[0, pl.ds(ROWS, ROWS)]),
                 (ln_gain, lng),
                 (w_query, wq),
                 (active, act),
@@ -107,7 +105,7 @@
     def _():
         for dz in (4, -4, 3, -3, 2, -2, 1, -1):
             greet(dev(dz=dz, core=1))
-        for dz in NEAR[::-1] + (-4,):
+        for dz in (4, -4, 3, -3, 2, -2, 1, -1, 0):
             greet(dev(dz=-dz, core=0))
         for e in (2, 1, 3):
             greet(dev(dy=e))
@@ -116,7 +114,7 @@
 
     @pl.when(c == 0)
     def _():
-        for dz in NEAR[::-1] + (-4,):
+        for dz in (4, -4, 3, -3, 2, -2, 1, -1, 0):
             greet(dev(dz=dz, core=1))
         for e in (2, 1, 3):
             greet(dev(dy=e))
@@ -124,7 +122,7 @@
 
     for n in range(4):
         loads[n].wait()
-    normed = layer_norm(fr[ROWS:, :], lng[...]).astype(BF16)
+    normed = layer_norm(fr[0, ROWS:, :], lng[...]).astype(BF16)
     qown[pl.ds(ROWS, ROWS), :] = jnp.dot(normed, wq[...], preferred_element_type=F32).astype(BF16)
 
     first = (z * NY + y) * 16
@@ -136,15 +134,37 @@
     keys_over = send(keys, kb.at[c], s_kv.at[0], r_kv.at[0], sibling)
     values_over = send(values, vb.at[c], s_kv.at[1], r_kv.at[1], sibling)
     query_over = send(qown.at[pl.ds(ROWS, ROWS)], qown.at[pl.ds(0, ROWS)], s_qx, r_qx, sibling)
-    frames_over = send(frames, fr.at[pl.ds(0, ROWS)], s_fr, r_fr, sibling)
+    frames_over = send(frames, fr.at[0, pl.ds(0, ROWS)], s_fr, r_fr, sibling)
+
     def slot(i):
         return qb.at[i // 2, 0, pl.ds((i % 2) * 2 * ROWS, 2 * ROWS)]
 
     query_out = [send(qown, slot(0), s_q.at[8], r_q.at[0], dev(dz=4, core=1))] + [
-        send(qown, slot(i), s_q.at[i], r_q.at[i], dev(dz=-NEAR[i], core=0)) for i in range(7, -1, -1)
+        send(qown, slot(i), s_q.at[i], r_q.at[i], dev(dz=-NEAR[i], core=0)) for i in (7, 3, 6, 2, 5, 1, 4, 0)
     ]
-    relay0 = [send(slot(7), slot(i), s_fw.at[i // 2], r_q.at[i], dev(dz=-(i // 2 + 1), core=1)) for i in (7, 5, 3, 1)]
-    relay1 = [send(slot(0), slot(i), s_fw.at[i // 2], r_q.at[i], dev(dz=i // 2, core=1)) for i in (6, 4, 2)]
+    relay0 = [
+        send(slot(7), slot(3 + n), s_fw.at[n - 1], r_q.at[3 + n], dev(dz=-n, core=1)) for n in (4, 3, 2, 1)
+    ]
+    relay1 = [send(slot(0), slot(n), s_fw.at[n - 1], r_q.at[n], dev(dz=n, core=1)) for n in (3, 2, 1)]
+
+    def pass_along():
+        @pl.when(c == 0)
+        def _():
+            arrived(slot(7), r_q.at[7])
+            for copy in relay0:
+                copy.start()
+
+        @pl.when(c == 1)
+        def _():
+            arrived(slot(0), r_q.at[0])
+            for copy in relay1:
+                copy.start()
+
+    def chunk(t):
+        return t + upper * (3 - 2 * t)
+
+    def forward(k, e):
+        return send(qb.at[k, 0], qb.at[k, NY - e], s_yf.at[k, e - 1], r_yf.at[k, NY - e - 1], dev(dy=e))
 
     sent0 += [query_over, frames_over]
     sent0 += relay0
@@ -170,33 +190,32 @@
     def _():
         frames_over.start()
 
-    @pl.when(c == 0)
-    def _():
-        arrived(slot(7), r_q.at[7])
-        for copy in relay0:
+    for t in range(4):
+        k = chunk(t)
+        if t in (0, 2):
+            pl.when(c + upper == 1 if t == 0 else c + upper != 1)(pass_along)
+        for j in (0, 1):
+            held = qb.at[k, 0, pl.ds(j * 2 * ROWS, 2 * ROWS)]
+            if t in (1, 2):
+                arrived(held, r_q.at[2 * k + j])
+            else:
+
+                @pl.when(2 * k + j != 7 - 7 * c)
+                def _():
+                    arrived(held, r_q.at[2 * k + j])
+
+        for e in (2, 1, 3):
+            forward(k, e).start()
+    sent += [forward(k, e) for k in range(4) for e in (1, 2, 3)]
+
+    frames_out = [send(fr.at[0], fr.at[NX - e], s_xf.at[e - 1], r_xf.at[NX - e - 1], dev(dx=e)) for e in (2, 1, 3)]
+    sent1 += frames_out
+
+    @pl.when(c == 1)
+    def _():
+        arrived(fr.at[0, pl.ds(0, ROWS)], r_fr)
+        for copy in frames_out:
             copy.start()
-        arrived(slot(0), r_q.at[0])
-
-    @pl.when(c == 1)
-    def _():
-        arrived(slot(0), r_q.at[0])
-        for copy in relay1:
-            copy.start()
-
-    for k in range(4):
-        for i in (2 * k, 2 * k + 1):
-            if 0 < i < 7:
-                arrived(slot(i), r_q.at[i])
-        if k == 3:
-
-            @pl.when(c == 1)
-            def _():
-                arrived(slot(7), r_q.at[7])
-
-        for e in (2, 1, 3):
-            copy = send(qb.at[k, 0], qb.at[k, NY - e], s_yf.at[k, e - 1], r_yf.at[k, NY - e - 1], dev(dy=e))
-            copy.start()
-            sent.append(copy)
 
     for n in range(4, 6):
         loads[n].wait()
@@ -208,7 +227,31 @@
 
     scale = 1.0 / (CAP * BIAS**0.5)
 
-    def attend(k, carry):
+    def to_owner(k, j):
+        i = 2 * k + j
+        up = i // 4
+        distance = up * (i - 3) - (1 - up) * i + (8 * up - 4) * c
+        return send(
+            zs.at[k, pl.ds(j * 2 * ROWS, 2 * ROWS)],
+            rz.at[c * 8 + i],
+            s_rz.at[i],
+            r_rz.at[c * 8 + i],
+            dev(dz=distance, core=1),
+        )
+
+    def add_up(t):
+        k = chunk(t)
+        total = po[k]
+        for e in (1, 3, 2):
+            arrived(ry.at[k, e - 1], r_ry.at[k, e - 1])
+            total = total + ry[k, e - 1].astype(F32)
+        zs[k] = total.astype(BF16)
+        for j in (1, 0):
+            to_owner(k, j).start()
+
+    def attend(t, carry):
+        k = chunk(t)
+        pl.when(t == 3)(lambda: add_up(0))
         for e in (1, 3, 2):
             arrived(qb.at[k, e], r_yf.at[k, e - 1])
         q = qb[k].reshape(STEP, BIAS)
@@ -236,81 +279,75 @@
     lax.fori_loop(0, 4, attend, 0)
     sent += [give_back(k, e) for k in range(4) for e in (1, 2, 3)]
 
-    for k in range(4):
-        total = po[k]
-        for e in (1, 3, 2):
-            arrived(ry.at[k, e - 1], r_ry.at[k, e - 1])
-            total = total + ry[k, e - 1].astype(F32)
-        zs[k] = total.astype(BF16)
-        for j in (1, 0):
-            i = 2 * k + j
-            copy = send(
-                zs.at[k, pl.ds(j * 2 * ROWS, 2 * ROWS)],
-                rz.at[c * 8 + i],
-                s_rz.at[i],
-                r_rz.at[c * 8 + i],
-                dev(dz=far(i), core=1),
-            )
-            copy.start()
-            sent.append(copy)
+    for t in range(1, 4):
+        add_up(t)
+    sent += [to_owner(k, j) for k in range(4) for j in (0, 1)]
 
     for n in range(6, 10):
         loads[n].wait()
 
-    residual_out = [
-        send(rs.at[0], rs.at[NX - e], s_xa.at[e - 1], r_xa.at[NX - e - 1], dev(dx=e)) for e in (2, 1, 3)
-    ]
+    half = D // 2
+    context_out = [send(cx.at[0], cx.at[NX - e], s_xa.at[e - 1], r_xa.at[NX - e - 1], dev(dx=e)) for e in (2, 1, 3)]
     residual_over = send(rs.at[0, pl.ds(0, ROWS)], rc, s_rc, r_rc, sibling)
     parts_out = [
-        send(
-            yo.at[e, pl.ds(core * ROWS, ROWS)],
-            xr.at[(NX - e) % NX],
-            s_xr.at[e * 2 + core],
-            r_xr.at[(NX - e) % NX],
-            dev(dx=e, core=core),
-        )
-        for e, core in ((2, 0), (2, 1), (1, 0), (1, 1), (3, 0), (3, 1), (0, 0))
+        [
+            send(
+                yo.at[h, e, pl.ds(core * ROWS, ROWS)],
+                xr.at[h, (NX - e) % NX],
+                s_xr.at[h, e * 2 + core],
+                r_xr.at[h, (NX - e) % NX],
+                dev(dx=e, core=core),
+            )
+            for e, core in ((2, 0), (2, 1), (1, 0), (1, 1), (3, 0), (3, 1), (0, 0))
+        ]
+        for h in (0, 1)
     ]
-
-    sent1 += residual_out + parts_out + [residual_over]
+    sent1 += context_out + parts_out[0] + parts_out[1] + [residual_over]
 
     @pl.when(c == 1)
     def _():
-        arrived(fr.at[pl.ds(0, ROWS)], r_fr)
+        for e in (1, 3, 2):
+            arrived(fr.at[e], r_xf.at[e - 1])
         total = jnp.zeros((2 * ROWS, WIDE), F32)
         for n in range(16):
             arrived(rz.at[n], r_rz.at[n])
             total = total + rz[n].astype(F32)
         context = total[:, :BIAS] / jnp.sum(total[:, BIAS:], axis=1, keepdims=True)
         power = jnp.mean(context * context, axis=1, keepdims=True)
-        context_norm = (context * lax.rsqrt(power + 0.0001)).astype(BF16)
-        residual = fr[...].astype(F32) + jnp.dot(context_norm, wo[...], preferred_element_type=F32)
-        rs[0] = residual.astype(BF16)
-        for copy in residual_out:
+        cx[0] = (context * lax.rsqrt(power + 0.0001)).astype(BF16)
+        for copy in context_out:
             copy.start()
+        for e in (1, 3, 2):
+            arrived(cx.at[e], r_xa.at[e - 1])
+        biased = jnp.dot(cx[...].reshape(NX * 2 * ROWS, BIAS), wo[...], preferred_element_type=F32)
+        residual = (fr[...].reshape(NX * 2 * ROWS, D).astype(F32) + biased).astype(BF16)
+        rs[...] = residual.reshape(NX, 2 * ROWS, D)
         residual_over.start()
-        for e in (1, 3, 2):
-            arrived(rs.at[e], r_xa.at[e - 1])
-        ffn_in = layer_norm(rs[...].reshape(NX * 2 * ROWS, D), ffg[...]).astype(BF16)
+        ffn_in = layer_norm(residual, ffg[...]).astype(BF16)
         hidden = gelu(jnp.dot(ffn_in, wu[...], preferred_element_type=F32)).astype(BF16)
-        part = jnp.dot(hidden, wd[...], preferred_element_type=F32).astype(BF16)
-        yo[...] = part.reshape(NX, 2 * ROWS, D)
-        for copy in parts_out:
-            copy.start()
-        done = rs[0, ROWS:, :].astype(F32) + yo[0, ROWS:, :].astype(F32)
-        for e in (1, 3, 2):
-            arrived(xr.at[e], r_xr.at[e])
-            done = done + xr[e].astype(F32)
-        out[...] = done.astype(BF16)
+        for h in (0, 1):
+            part = jnp.dot(hidden, wd[:, h * half : (h + 1) * half], preferred_element_type=F32)
+            yo[h] = part.astype(BF16).reshape(NX, 2 * ROWS, half)
+            for copy in parts_out[h]:
+                copy.start()
+        for h in (0, 1):
+            cols = slice(h * half, (h + 1) * half)
+            done = rs[0, ROWS:, cols].astype(F32) + yo[h, 0, ROWS:, :].astype(F32)
+            for e in (1, 3, 2):
+                arrived(xr.at[h, e], r_xr.at[h, e])
+                done = done + xr[h, e].astype(F32)
+            out[:, cols] = done.astype(BF16)
 
     @pl.when(c == 0)
     def _():
         arrived(rc, r_rc)
-        done = rc[...].astype(F32)
-        for e in (0, 1, 3, 2):
-            arrived(xr.at[e], r_xr.at[e])
-            done = done + xr[e].astype(F32)
-        out[...] = done.astype(BF16)
+        for h in (0, 1):
+            cols = slice(h * half, (h + 1) * half)
+            done = rc[:, cols].astype(F32)
+            for e in (0, 1, 3, 2):
+                arrived(xr.at[h, e], r_xr.at[h, e])
+                done = done + xr[h, e].astype(F32)
+            out[:, cols] = done.astype(BF16)
 
     finish()
 
@@ -325,7 +362,7 @@
         in_specs=[pl.BlockSpec(memory_space=pltpu.HBM)] * 10,
         out_specs=pl.BlockSpec(memory_space=pltpu.VMEM),
         scratch_shapes=[
-            vm((rows, D), BF16),
+            vm((NX, rows, D), BF16),
             vm((D,), F32),
             vm((D,), F32),
             vm((D, BIAS), BF16),
@@ -342,9 +379,10 @@
             vm((4, 3, 2 * rows, WIDE), BF16),
             vm((4, 2 * rows, WIDE), BF16),
             vm((16, rows, WIDE), BF16),
+            vm((NX, rows, BIAS), BF16),
             vm((NX, rows, D), BF16),
-            vm((NX, rows, D), BF16),
-            vm((NX, ROWS, D), BF16),
+            vm((2, NX, rows, D // 2), BF16),
+            vm((2, NX, ROWS, D // 2), BF16),
             vm((ROWS, D), BF16),
             vm((16, 128), F32),
             vm((STEP, 2 * PH), BF16),
@@ -357,7 +395,8 @@
             dma((4, 3)), dma((4, 3)),
             dma((8,)), dma((16,)),
             dma((3,)), dma((3,)),
-            dma((8,)), dma((4,)),
+            dma((3,)), dma((3,)),
+            dma((2, 8)), dma((2, 4)),
             dma, dma,
         ],
         compiler_params=pltpu.CompilerParams(

time: 59.8 us -> 55.2 us (0.923)
  Pallas kernels: 58.2 us -> 53.6 us
    pallas_call x1, Pallas kernels: 58.2 us -> 53.6 us  [local(): pl.pallas_call(kernel, out_shape=jax.ShapeDtypeStruct((ROWS, D), BF16), i...]
where the time goes in v3:
time: 55.2 us; the launch traced here: 55 us
  Pallas kernels  53.6 us (97%)
  local copies, waits for them, and re-layouts  1.4 us (3%)
    pallas_call x1, Pallas kernels, local(): pl.pallas_call(kernel, out_shape=jax.ShapeDtypeStruct((ROWS, D), BF16), i...  53.6 us
    unnamed x1, local copies, waits for them, and re-layouts  1.4 us

profile of v3, /device:TPU:1, one launch (start us, length us, event | category | flops | bytes accessed | tf_op | source)
XLA Modules:
  0.0 55.0 jit_solution(4765562531554436556)
XLA Ops:
  0.0 53.6 %layer.1 = bf16[16,1280]{1,0:T(8,128)(2,1)} custom-call(bf16[16,1280]{1,0:T(8,128)(2,1)} %frames.1, f32[1280]{0:T(1024)} %ln_gain.1, bf16[1280,256]{1,0:T(8,128)(2,1)} %w_query.1, bf16[1024,256]{1,0:T(8,128)(2,1)} %keys.1, bf16[1024,256]{1,0:T(8,128)(2,1)} %values.1, s32[4,256]{1,0:T(4,128)} %active.1, bf16[256,1280]{1,0:T(8,128)(2,1)} %w_out.1, ...), custom_call_target="tpu_custom_call" | custom-call | tf_op jit(solution)/shard_map/layer/pallas_call | solution.py:359
  53.6 1.4 %copy.12 = bf16[16,1280]{1,0:T(8,128)(2,1)} copy(bf16[16,1280]{1,0:T(8,128)(2,1)} %layer.1) | data formatting | bytes 81920

commit v4 on v3

--- a/solution.py
+++ b/solution.py
@@ -15,7 +15,6 @@
 D, FFL, BIAS = 1280, 640, 256
 ROWS = 16
 PH = 1024
-WIDE = BIAS + 128
 STEP = 256
 
 
@@ -34,9 +33,9 @@
 def kernel(
     frames, ln_gain, w_query, keys, values, active, w_out, ffn_gain, w_up, w_down, out,
     fr, lng, ffg, wq, kb, vb, act, wo, wu, wd,
-    qown, qb, pb, po, ry, zs, rz, cx, rs, yo, xr, rc, bias, wb,
+    qown, qb, pb, po, ry, zs, rz, ty, tr, ts, tz, cx, rs, yo, xr, rc, bias, wb,
     ld, s_kv, r_kv, s_fr, r_fr, s_qx, r_qx, s_q, r_q, s_fw, s_yf, r_yf, s_ry, r_ry, s_rz, r_rz,
-    s_xf, r_xf, s_xa, r_xa, s_xr, r_xr, s_rc, r_rc,
+    s_ty, r_ty, s_tz, r_tz, s_xf, r_xf, s_xa, r_xa, s_xr, r_xr, s_rc, r_rc,
 ):
     x = lax.axis_index("dp")
     b = lax.axis_index("bank")
@@ -129,6 +128,7 @@
     ids = first + lax.broadcasted_iota(jnp.int32, (16, 256), 0)
     hits = jnp.where(ids == act[pl.ds(x, 1), :], 1.0, 0.0).astype(F32)
     found = jnp.max(hits, axis=1, keepdims=True)
+    ty[...] = jnp.zeros_like(ty)
     bias[...] = jnp.broadcast_to(jnp.where(found > 0.5, 0.0, -512.0).astype(F32), (16, 128))
 
     keys_over = send(keys, kb.at[c], s_kv.at[0], r_kv.at[0], sibling)
@@ -267,20 +267,39 @@
             wb[:, p * STEP : (p + 1) * STEP] = weight.astype(BF16)
         num = jnp.dot(wb[...], vb[...].reshape(2 * PH, BIAS), preferred_element_type=F32)
         part = 4 * ROWS
-        po[k, :, :BIAS] = num[:part]
-        po[k, :, BIAS:] = tot[:part]
-        for e in (1, 2, 3):
-            pb[k, e - 1, :, :BIAS] = num[e * part : (e + 1) * part].astype(BF16)
-            pb[k, e - 1, :, BIAS:] = tot[e * part : (e + 1) * part].astype(BF16)
+        po[k] = num[:part]
         for e in (2, 1, 3):
+            pb[k, e - 1] = num[e * part : (e + 1) * part].astype(BF16)
             give_back(k, e).start()
+        row = lax.dot_general(
+            jnp.ones((8, 128), BF16), tot.astype(BF16), (((1,), (1,)), ((), ())), preferred_element_type=F32
+        )
+        for e in range(NY):
+            ty[e, k, :, :part] = row[:1, e * part : (e + 1) * part]
         return carry
 
     lax.fori_loop(0, 4, attend, 0)
     sent += [give_back(k, e) for k in range(4) for e in (1, 2, 3)]
 
+    totals_back = [send(ty.at[e], tr.at[NY - e - 1], s_ty.at[e - 1], r_ty.at[NY - e - 1], dev(dy=e)) for e in (2, 1, 3)]
+    for copy in totals_back:
+        copy.start()
+    sent += totals_back
+
     for t in range(1, 4):
         add_up(t)
+    totals = ty[0]
+    for e in (1, 3, 2):
+        arrived(tr.at[e - 1], r_ty.at[e - 1])
+        totals = totals + tr[e - 1]
+    ts[...] = totals
+    totals_out = [
+        send(ts.at[i // 2], tz.at[c * 8 + i], s_tz.at[i], r_tz, dev(dz=NEAR[i] + (-4 if i < 4 else 4) * c, core=1))
+        for i in (7, 3, 6, 2, 5, 1, 4, 0)
+    ]
+    for copy in totals_out:
+        copy.start()
+    sent += totals_out
     sent += [to_owner(k, j) for k in range(4) for j in (0, 1)]
 
     for n in range(6, 10):
@@ -308,11 +327,17 @@
     def _():
         for e in (1, 3, 2):
             arrived(fr.at[e], r_xf.at[e - 1])
-        total = jnp.zeros((2 * ROWS, WIDE), F32)
+        total = jnp.zeros((2 * ROWS, BIAS), F32)
         for n in range(16):
             arrived(rz.at[n], r_rz.at[n])
             total = total + rz[n].astype(F32)
-        context = total[:, :BIAS] / jnp.sum(total[:, BIAS:], axis=1, keepdims=True)
+        arrived(tz, r_tz)
+        even, odd = tz[0], tz[1]
+        for n in range(2, 16, 2):
+            even, odd = even + tz[n], odd + tz[n + 1]
+        gap = lax.broadcasted_iota(jnp.int32, (2 * ROWS, 128), 1) - lax.broadcasted_iota(jnp.int32, (2 * ROWS, 128), 0)
+        spread = jnp.where(gap == 0, even, 0.0) + jnp.where(gap == 2 * ROWS, odd, 0.0)
+        context = total / jnp.sum(spread, axis=1, keepdims=True)
         power = jnp.mean(context * context, axis=1, keepdims=True)
         cx[0] = (context * lax.rsqrt(power + 0.0001)).astype(BF16)
         for copy in context_out:
@@ -374,11 +399,15 @@
             vm((FFL, D), BF16),
             vm((rows, BIAS), BF16),
             vm((4, NY, 2 * rows, BIAS), BF16),
-            vm((4, 3, 2 * rows, WIDE), BF16),
-            vm((4, 2 * rows, WIDE), F32),
-            vm((4, 3, 2 * rows, WIDE), BF16),
-            vm((4, 2 * rows, WIDE), BF16),
-            vm((16, rows, WIDE), BF16),
+            vm((4, 3, 2 * rows, BIAS), BF16),
+            vm((4, 2 * rows, BIAS), F32),
+            vm((4, 3, 2 * rows, BIAS), BF16),
+            vm((4, 2 * rows, BIAS), BF16),
+            vm((16, rows, BIAS), BF16),
+            vm((NY, 4, 1, 128), F32),
+            vm((3, 4, 1, 128), F32),
+            vm((4, 1, 128), F32),
+            vm((16, 1, 128), F32),
             vm((NX, rows, BIAS), BF16),
             vm((NX, rows, D), BF16),
             vm((2, NX, rows, D // 2), BF16),
@@ -395,6 +424,8 @@
             dma((4, 3)), dma((4, 3)),
             dma((8,)), dma((16,)),
             dma((3,)), dma((3,)),
+            dma((8,)), dma,
+            dma((3,)), dma((3,)),
             dma((3,)), dma((3,)),
             dma((2, 8)), dma((2, 4)),
             dma, dma,

time: 55.2 us -> 54.5 us (0.987)
  Pallas kernels: 53.6 us -> 52.6 us
    pallas_call x1, Pallas kernels: 53.6 us -> 52.6 us  [local(): pl.pallas_call(kernel, out_shape=jax.ShapeDtypeStruct((ROWS, D), BF16), i...]
where the time goes in v4:
time: 54.5 us; the launch traced here: 54.1 us
  Pallas kernels  52.6 us (97%)
  local copies, waits for them, and re-layouts  1.4 us (3%)
    pallas_call x1, Pallas kernels, local(): pl.pallas_call(kernel, out_shape=jax.ShapeDtypeStruct((ROWS, D), BF16), i...  52.6 us
    unnamed x1, local copies, waits for them, and re-layouts  1.4 us

profile of v4, /device:TPU:1, one launch (start us, length us, event | category | flops | bytes accessed | tf_op | source)
XLA Modules:
  0.0 54.1 jit_solution(3670353141671819895)
XLA Ops:
  0.0 52.6 %layer.1 = bf16[16,1280]{1,0:T(8,128)(2,1)} custom-call(bf16[16,1280]{1,0:T(8,128)(2,1)} %frames.1, f32[1280]{0:T(1024)} %ln_gain.1, bf16[1280,256]{1,0:T(8,128)(2,1)} %w_query.1, bf16[1024,256]{1,0:T(8,128)(2,1)} %keys.1, bf16[1024,256]{1,0:T(8,128)(2,1)} %values.1, s32[4,256]{1,0:T(4,128)} %active.1, bf16[256,1280]{1,0:T(8,128)(2,1)} %w_out.1, ...), custom_call_target="tpu_custom_call" | custom-call | tf_op jit(solution)/shard_map/layer/pallas_call | solution.py:384
  52.7 1.4 %copy.12 = bf16[16,1280]{1,0:T(8,128)(2,1)} copy(bf16[16,1280]{1,0:T(8,128)(2,1)} %layer.1) | data formatting | bytes 81920

commit v5 on v4

--- a/solution.py
+++ b/solution.py
@@ -10,7 +10,8 @@
 BF16 = jnp.bfloat16
 CAP = 30.0
 LOG2E = 1.4426950408889634
-NEAR = (0, -1, -2, -3, 1, 2, 3, 4)
+NEAR = (0, 1, -1, 2, -2, 3, -3, 4)
+FAR = (-4, 5, -5, 6, -6, 7, -7, 8)
 NZ, NY, NX = 16, 4, 4
 D, FFL, BIAS = 1280, 640, 256
 ROWS = 16
@@ -33,8 +34,8 @@
 def kernel(
     frames, ln_gain, w_query, keys, values, active, w_out, ffn_gain, w_up, w_down, out,
     fr, lng, ffg, wq, kb, vb, act, wo, wu, wd,
-    qown, qb, pb, po, ry, zs, rz, ty, tr, ts, tz, cx, rs, yo, xr, rc, bias, wb,
-    ld, s_kv, r_kv, s_fr, r_fr, s_qx, r_qx, s_q, r_q, s_fw, s_yf, r_yf, s_ry, r_ry, s_rz, r_rz,
+    qown, qb, pb, po, ry, zs, rz, ty, tr, ts, tz, cx, rs, yo, xr, rc, bias, wb, upper,
+    ld, s_kv, r_kv, s_fr, r_fr, s_qx, r_qx, s_q, r_q, r_up, s_fw, s_yf, r_yf, s_ry, r_ry, s_rz, r_rz,
     s_ty, r_ty, s_tz, r_tz, s_xf, r_xf, s_xa, r_xa, s_xr, r_xr, s_rc, r_rc,
 ):
     x = lax.axis_index("dp")
@@ -42,7 +43,6 @@
     c = lax.rem(b, 2)
     y = lax.rem(b // 2, NY)
     z = b // (2 * NY)
-    upper = z // (NZ // 2)
 
     def dev(dx=0, dz=0, dy=0, core=None):
         cz = lax.rem(z + dz + 2 * NZ, NZ)
@@ -76,7 +76,7 @@
             )
         )
     ]
-    for load in loads:
+    for load in loads[:4]:
         load.start()
 
     sent, sent0, sent1 = [], [], []
@@ -104,7 +104,7 @@
     def _():
         for dz in (4, -4, 3, -3, 2, -2, 1, -1):
             greet(dev(dz=dz, core=1))
-        for dz in (4, -4, 3, -3, 2, -2, 1, -1, 0):
+        for dz in NEAR[::-1]:
             greet(dev(dz=-dz, core=0))
         for e in (2, 1, 3):
             greet(dev(dy=e))
@@ -113,7 +113,7 @@
 
     @pl.when(c == 0)
     def _():
-        for dz in (4, -4, 3, -3, 2, -2, 1, -1, 0):
+        for dz in NEAR[::-1]:
             greet(dev(dz=dz, core=1))
         for e in (2, 1, 3):
             greet(dev(dy=e))
@@ -121,6 +121,8 @@
 
     for n in range(4):
         loads[n].wait()
+    for load in loads[4:]:
+        load.start()
     normed = layer_norm(fr[0, ROWS:, :], lng[...]).astype(BF16)
     qown[pl.ds(ROWS, ROWS), :] = jnp.dot(normed, wq[...], preferred_element_type=F32).astype(BF16)
 
@@ -139,46 +141,32 @@
     def slot(i):
         return qb.at[i // 2, 0, pl.ds((i % 2) * 2 * ROWS, 2 * ROWS)]
 
-    query_out = [send(qown, slot(0), s_q.at[8], r_q.at[0], dev(dz=4, core=1))] + [
-        send(qown, slot(i), s_q.at[i], r_q.at[i], dev(dz=-NEAR[i], core=0)) for i in (7, 3, 6, 2, 5, 1, 4, 0)
+    query_out = [
+        send(qown, upper, s_q.at[9], r_up, dev(dz=-4, core=1)),
+        send(qown, slot(0), s_q.at[8], r_q.at[0], dev(dz=4, core=1)),
+    ] + [
+        send(qown, slot(i), s_q.at[i], r_q.at[i], dev(dz=-NEAR[i], core=0)) for i in range(7, -1, -1)
     ]
-    relay0 = [
-        send(slot(7), slot(3 + n), s_fw.at[n - 1], r_q.at[3 + n], dev(dz=-n, core=1)) for n in (4, 3, 2, 1)
+    relay_down = [
+        send(upper, slot(2 * n - 1), s_fw.at[2 * n - 1], r_q.at[2 * n - 1], dev(dz=-n, core=1)) for n in (4, 3, 2, 1)
     ]
-    relay1 = [send(slot(0), slot(n), s_fw.at[n - 1], r_q.at[n], dev(dz=n, core=1)) for n in (3, 2, 1)]
-
-    def pass_along():
-        @pl.when(c == 0)
-        def _():
-            arrived(slot(7), r_q.at[7])
-            for copy in relay0:
-                copy.start()
-
-        @pl.when(c == 1)
-        def _():
-            arrived(slot(0), r_q.at[0])
-            for copy in relay1:
-                copy.start()
-
-    def chunk(t):
-        return t + upper * (3 - 2 * t)
+    relay_up = [send(slot(0), slot(2 * n), s_fw.at[2 * n], r_q.at[2 * n], dev(dz=n, core=1)) for n in (3, 2, 1)]
 
     def forward(k, e):
         return send(qb.at[k, 0], qb.at[k, NY - e], s_yf.at[k, e - 1], r_yf.at[k, NY - e - 1], dev(dy=e))
 
     sent0 += [query_over, frames_over]
-    sent0 += relay0
-    sent1 += query_out + relay1
+    sent1 += query_out + relay_down + relay_up
     sent += [keys_over, values_over]
 
     @pl.when(c == 0)
     def _():
-        pl.semaphore_wait(barrier, 15)
+        pl.semaphore_wait(barrier, 14)
         query_over.start()
 
     @pl.when(c == 1)
     def _():
-        pl.semaphore_wait(barrier, 26)
+        pl.semaphore_wait(barrier, 25)
         arrived(qown.at[pl.ds(0, ROWS)], r_qx)
         for copy in query_out:
             copy.start()
@@ -190,20 +178,23 @@
     def _():
         frames_over.start()
 
-    for t in range(4):
-        k = chunk(t)
-        if t in (0, 2):
-            pl.when(c + upper == 1 if t == 0 else c + upper != 1)(pass_along)
-        for j in (0, 1):
-            held = qb.at[k, 0, pl.ds(j * 2 * ROWS, 2 * ROWS)]
-            if t in (1, 2):
-                arrived(held, r_q.at[2 * k + j])
-            else:
-
-                @pl.when(2 * k + j != 7 - 7 * c)
-                def _():
-                    arrived(held, r_q.at[2 * k + j])
-
+    @pl.when(c == 1)
+    def _():
+        arrived(upper, r_up)
+        for copy in relay_down:
+            copy.start()
+
+    arrived(slot(0), r_q.at[0])
+
+    @pl.when(c == 1)
+    def _():
+        for copy in relay_up:
+            copy.start()
+
+    for k in range(4):
+        for i in (2 * k, 2 * k + 1):
+            if i:
+                arrived(slot(i), r_q.at[i])
         for e in (2, 1, 3):
             forward(k, e).start()
     sent += [forward(k, e) for k in range(4) for e in (1, 2, 3)]
@@ -227,20 +218,16 @@
 
     scale = 1.0 / (CAP * BIAS**0.5)
 
+    def owner(i):
+        return dev(dz=NEAR[i] + (FAR[i] - NEAR[i]) * c, core=1)
+
     def to_owner(k, j):
         i = 2 * k + j
-        up = i // 4
-        distance = up * (i - 3) - (1 - up) * i + (8 * up - 4) * c
         return send(
-            zs.at[k, pl.ds(j * 2 * ROWS, 2 * ROWS)],
-            rz.at[c * 8 + i],
-            s_rz.at[i],
-            r_rz.at[c * 8 + i],
-            dev(dz=distance, core=1),
+            zs.at[k, pl.ds(j * 2 * ROWS, 2 * ROWS)], rz.at[c * 8 + i], s_rz.at[i], r_rz.at[c * 8 + i], owner(i)
         )
 
-    def add_up(t):
-        k = chunk(t)
+    def add_up(k):
         total = po[k]
         for e in (1, 3, 2):
             arrived(ry.at[k, e - 1], r_ry.at[k, e - 1])
@@ -249,9 +236,8 @@
         for j in (1, 0):
             to_owner(k, j).start()
 
-    def attend(t, carry):
-        k = chunk(t)
-        pl.when(t == 3)(lambda: add_up(0))
+    def attend(k, carry):
+        pl.when((k == 3) & (c == 0))(lambda: add_up(0))
         for e in (1, 3, 2):
             arrived(qb.at[k, e], r_yf.at[k, e - 1])
         q = qb[k].reshape(STEP, BIAS)
@@ -286,16 +272,17 @@
         copy.start()
     sent += totals_back
 
-    for t in range(1, 4):
-        add_up(t)
+    pl.when(c == 1)(lambda: add_up(0))
+    for k in range(1, 4):
+        add_up(k)
     totals = ty[0]
     for e in (1, 3, 2):
         arrived(tr.at[e - 1], r_ty.at[e - 1])
         totals = totals + tr[e - 1]
     ts[...] = totals
     totals_out = [
-        send(ts.at[i // 2], tz.at[c * 8 + i], s_tz.at[i], r_tz, dev(dz=NEAR[i] + (-4 if i < 4 else 4) * c, core=1))
-        for i in (7, 3, 6, 2, 5, 1, 4, 0)
+        send(ts.at[i // 2], tz.at[c * 8 + i], s_tz.at[i], r_tz, owner(i))
+        for i in range(7, -1, -1)
     ]
     for copy in totals_out:
         copy.start()
@@ -415,11 +402,12 @@
             vm((ROWS, D), BF16),
             vm((16, 128), F32),
             vm((STEP, 2 * PH), BF16),
+            vm((rows, BIAS), BF16),
             dma((10,)),
             dma((2,)), dma((2,)),
             dma, dma,
             dma, dma,
-            dma((9,)), dma((8,)), dma((4,)),
+            dma((10,)), dma((8,)), dma, dma((8,)),
             dma((4, 3)), dma((4, 3)),
             dma((4, 3)), dma((4, 3)),
             dma((8,)), dma((16,)),

time: 54.5 us -> 54 us (level)
  no operation moved by 1% of the time
where the time goes in v5:
time: 54 us; the launch traced here: 53.8 us
  Pallas kernels  52.4 us (97%)
  local copies, waits for them, and re-layouts  1.4 us (3%)
    pallas_call x1, Pallas kernels, local(): pl.pallas_call(kernel, out_shape=jax.ShapeDtypeStruct((ROWS, D), BF16), i...  52.4 us
    unnamed x1, local copies, waits for them, and re-layouts  1.4 us

profile of v5, /device:TPU:1, one launch (start us, length us, event | category | flops | bytes accessed | tf_op | source)
XLA Modules:
  0.0 53.8 jit_solution(8163173776416338888)
XLA Ops:
  0.0 52.4 %layer.1 = bf16[16,1280]{1,0:T(8,128)(2,1)} custom-call(bf16[16,1280]{1,0:T(8,128)(2,1)} %frames.1, f32[1280]{0:T(1024)} %ln_gain.1, bf16[1280,256]{1,0:T(8,128)(2,1)} %w_query.1, bf16[1024,256]{1,0:T(8,128)(2,1)} %keys.1, bf16[1024,256]{1,0:T(8,128)(2,1)} %values.1, s32[4,256]{1,0:T(4,128)} %active.1, bf16[256,1280]{1,0:T(8,128)(2,1)} %w_out.1, ...), custom_call_target="tpu_custom_call" | custom-call | tf_op jit(solution)/shard_map/layer/pallas_call | solution.py:371
  52.4 1.4 %copy.12 = bf16[16,1280]{1,0:T(8,128)(2,1)} copy(bf16[16,1280]{1,0:T(8,128)(2,1)} %layer.1) | data formatting | bytes 81920

commit v6 on v5

--- a/solution.py
+++ b/solution.py
@@ -102,21 +102,19 @@
 
     @pl.when(c == 1)
     def _():
+        greet(sibling)
         for dz in (4, -4, 3, -3, 2, -2, 1, -1):
-            greet(dev(dz=dz, core=1))
-        for dz in NEAR[::-1]:
-            greet(dev(dz=-dz, core=0))
+            greet(dev(dz=dz))
         for e in (2, 1, 3):
             greet(dev(dy=e))
-            greet(dev(dx=e, core=0))
-            greet(dev(dx=e, core=1))
+            greet(dev(dx=e))
 
     @pl.when(c == 0)
     def _():
         for dz in NEAR[::-1]:
             greet(dev(dz=dz, core=1))
         for e in (2, 1, 3):
-            greet(dev(dy=e))
+            greet(dev(dy=e, core=1))
             greet(dev(dx=e, core=1))
 
     for n in range(4):
@@ -161,12 +159,12 @@
 
     @pl.when(c == 0)
     def _():
-        pl.semaphore_wait(barrier, 14)
+        pl.semaphore_wait(barrier, 1)
         query_over.start()
 
     @pl.when(c == 1)
     def _():
-        pl.semaphore_wait(barrier, 25)
+        pl.semaphore_wait(barrier, 28)
         arrived(qown.at[pl.ds(0, ROWS)], r_qx)
         for copy in query_out:
             copy.start()

time: 54 us -> 53.4 us (0.989)
  Pallas kernels: 52.4 us -> 51.8 us
    pallas_call x1, Pallas kernels: 52.4 us -> 51.8 us  [local(): pl.pallas_call(kernel, out_shape=jax.ShapeDtypeStruct((ROWS, D), BF16), i...]
where the time goes in v6:
time: 53.4 us; the launch traced here: 53.2 us
  Pallas kernels  51.8 us (97%)
  local copies, waits for them, and re-layouts  1.4 us (3%)
    pallas_call x1, Pallas kernels, local(): pl.pallas_call(kernel, out_shape=jax.ShapeDtypeStruct((ROWS, D), BF16), i...  51.8 us
    unnamed x1, local copies, waits for them, and re-layouts  1.4 us

profile of v6, /device:TPU:1, one launch (start us, length us, event | category | flops | bytes accessed | tf_op | source)
XLA Modules:
  0.0 53.2 jit_solution(1143525910220429375)
XLA Ops:
  0.0 51.8 %layer.1 = bf16[16,1280]{1,0:T(8,128)(2,1)} custom-call(bf16[16,1280]{1,0:T(8,128)(2,1)} %frames.1, f32[1280]{0:T(1024)} %ln_gain.1, bf16[1280,256]{1,0:T(8,128)(2,1)} %w_query.1, bf16[1024,256]{1,0:T(8,128)(2,1)} %keys.1, bf16[1024,256]{1,0:T(8,128)(2,1)} %values.1, s32[4,256]{1,0:T(4,128)} %active.1, bf16[256,1280]{1,0:T(8,128)(2,1)} %w_out.1, ...), custom_call_target="tpu_custom_call" | custom-call | tf_op jit(solution)/shard_map/layer/pallas_call | solution.py:369
  51.8 1.4 %copy.12 = bf16[16,1280]{1,0:T(8,128)(2,1)} copy(bf16[16,1280]{1,0:T(8,128)(2,1)} %layer.1) | data formatting | bytes 81920

commit v7 on v6

--- a/solution.py
+++ b/solution.py
@@ -35,7 +35,7 @@
     frames, ln_gain, w_query, keys, values, active, w_out, ffn_gain, w_up, w_down, out,
     fr, lng, ffg, wq, kb, vb, act, wo, wu, wd,
     qown, qb, pb, po, ry, zs, rz, ty, tr, ts, tz, cx, rs, yo, xr, rc, bias, wb, upper,
-    ld, s_kv, r_kv, s_fr, r_fr, s_qx, r_qx, s_q, r_q, r_up, s_fw, s_yf, r_yf, s_ry, r_ry, s_rz, r_rz,
+    ld, s_kv, r_kv, s_fr, r_fr, s_q, r_q, r_up, s_fw, s_yf, r_yf, s_ry, r_ry, s_rz, r_rz,
     s_ty, r_ty, s_tz, r_tz, s_xf, r_xf, s_xa, r_xa, s_xr, r_xr, s_rc, r_rc,
 ):
     x = lax.axis_index("dp")
@@ -117,23 +117,8 @@
             greet(dev(dy=e, core=1))
             greet(dev(dx=e, core=1))
 
-    for n in range(4):
-        loads[n].wait()
-    for load in loads[4:]:
-        load.start()
-    normed = layer_norm(fr[0, ROWS:, :], lng[...]).astype(BF16)
-    qown[pl.ds(ROWS, ROWS), :] = jnp.dot(normed, wq[...], preferred_element_type=F32).astype(BF16)
-
-    first = (z * NY + y) * 16
-    ids = first + lax.broadcasted_iota(jnp.int32, (16, 256), 0)
-    hits = jnp.where(ids == act[pl.ds(x, 1), :], 1.0, 0.0).astype(F32)
-    found = jnp.max(hits, axis=1, keepdims=True)
-    ty[...] = jnp.zeros_like(ty)
-    bias[...] = jnp.broadcast_to(jnp.where(found > 0.5, 0.0, -512.0).astype(F32), (16, 128))
-
     keys_over = send(keys, kb.at[c], s_kv.at[0], r_kv.at[0], sibling)
     values_over = send(values, vb.at[c], s_kv.at[1], r_kv.at[1], sibling)
-    query_over = send(qown.at[pl.ds(ROWS, ROWS)], qown.at[pl.ds(0, ROWS)], s_qx, r_qx, sibling)
     frames_over = send(frames, fr.at[0, pl.ds(0, ROWS)], s_fr, r_fr, sibling)
 
     def slot(i):
@@ -153,28 +138,43 @@
     def forward(k, e):
         return send(qb.at[k, 0], qb.at[k, NY - e], s_yf.at[k, e - 1], r_yf.at[k, NY - e - 1], dev(dy=e))
 
-    sent0 += [query_over, frames_over]
+    sent0 += [frames_over]
     sent1 += query_out + relay_down + relay_up
     sent += [keys_over, values_over]
 
     @pl.when(c == 0)
     def _():
         pl.semaphore_wait(barrier, 1)
-        query_over.start()
-
-    @pl.when(c == 1)
-    def _():
+        frames_over.start()
+        for load in loads[4:]:
+            load.start()
+        for load in loads[:3]:
+            load.wait()
+
+    @pl.when(c == 1)
+    def _():
+        loads[0].wait()
+        loads[1].wait()
+        arrived(fr.at[0, pl.ds(0, ROWS)], r_fr)
+        normed = layer_norm(fr[0], lng[...]).astype(BF16)
+        loads[2].wait()
+        qown[...] = jnp.dot(normed, wq[...], preferred_element_type=F32).astype(BF16)
+        for load in loads[4:]:
+            load.start()
         pl.semaphore_wait(barrier, 28)
-        arrived(qown.at[pl.ds(0, ROWS)], r_qx)
         for copy in query_out:
             copy.start()
 
     keys_over.start()
     values_over.start()
 
-    @pl.when(c == 0)
-    def _():
-        frames_over.start()
+    loads[3].wait()
+    first = (z * NY + y) * 16
+    ids = first + lax.broadcasted_iota(jnp.int32, (16, 256), 0)
+    hits = jnp.where(ids == act[pl.ds(x, 1), :], 1.0, 0.0).astype(F32)
+    found = jnp.max(hits, axis=1, keepdims=True)
+    bias[...] = jnp.broadcast_to(jnp.where(found > 0.5, 0.0, -512.0).astype(F32), (16, 128))
+    ty[...] = jnp.zeros_like(ty)
 
     @pl.when(c == 1)
     def _():
@@ -202,7 +202,6 @@
 
     @pl.when(c == 1)
     def _():
-        arrived(fr.at[0, pl.ds(0, ROWS)], r_fr)
         for copy in frames_out:
             copy.start()
 
@@ -233,6 +232,28 @@
         zs[k] = total.astype(BF16)
         for j in (1, 0):
             to_owner(k, j).start()
+
+    spans = (pl.ds(0, 3), pl.ds(3, 1))
+    totals_back = [
+        [
+            send(ty.at[e, span], tr.at[NY - e - 1, span], s_ty.at[n, e - 1], r_ty.at[n, NY - e - 1], dev(dy=e))
+            for e in (2, 1, 3)
+        ]
+        for n, span in enumerate(spans)
+    ]
+    totals_out = [
+        send(ts.at[i // 2], tz.at[c * 8 + i], s_tz.at[i], r_tz, owner(i)) for i in range(8)
+    ]
+
+    def add_totals(n):
+        span = spans[n]
+        totals = ty[0, span]
+        for e in (1, 3, 2):
+            arrived(tr.at[e - 1, span], r_ty.at[n, e - 1])
+            totals = totals + tr[e - 1, span]
+        ts[span] = totals
+        for copy in totals_out[6:] if n else totals_out[:6]:
+            copy.start()
 
     def attend(k, carry):
         pl.when((k == 3) & (c == 0))(lambda: add_up(0))
@@ -260,30 +281,27 @@
         )
         for e in range(NY):
             ty[e, k, :, :part] = row[:1, e * part : (e + 1) * part]
+
+        @pl.when(k == 2)
+        def _():
+            for copy in totals_back[0]:
+                copy.start()
+
         return carry
 
     lax.fori_loop(0, 4, attend, 0)
     sent += [give_back(k, e) for k in range(4) for e in (1, 2, 3)]
 
-    totals_back = [send(ty.at[e], tr.at[NY - e - 1], s_ty.at[e - 1], r_ty.at[NY - e - 1], dev(dy=e)) for e in (2, 1, 3)]
-    for copy in totals_back:
+    for copy in totals_back[1]:
         copy.start()
-    sent += totals_back
+    sent += totals_back[0] + totals_back[1]
 
     pl.when(c == 1)(lambda: add_up(0))
-    for k in range(1, 4):
-        add_up(k)
-    totals = ty[0]
-    for e in (1, 3, 2):
-        arrived(tr.at[e - 1], r_ty.at[e - 1])
-        totals = totals + tr[e - 1]
-    ts[...] = totals
-    totals_out = [
-        send(ts.at[i // 2], tz.at[c * 8 + i], s_tz.at[i], r_tz, owner(i))
-        for i in range(7, -1, -1)
-    ]
-    for copy in totals_out:
-        copy.start()
+    add_up(1)
+    add_up(2)
+    add_totals(0)
+    add_up(3)
+    add_totals(1)
     sent += totals_out
     sent += [to_owner(k, j) for k in range(4) for j in (0, 1)]
 
@@ -404,12 +422,11 @@
             dma((10,)),
             dma((2,)), dma((2,)),
             dma, dma,
-            dma, dma,
             dma((10,)), dma((8,)), dma, dma((8,)),
             dma((4, 3)), dma((4, 3)),
             dma((4, 3)), dma((4, 3)),
             dma((8,)), dma((16,)),
-            dma((3,)), dma((3,)),
+            dma((2, 3)), dma((2, 3)),
             dma((8,)), dma,
             dma((3,)), dma((3,)),
             dma((3,)), dma((3,)),

time: 53.4 us -> 53.7 us (level)
  no operation moved by 1% of the time
where the time goes in v7:
time: 53.7 us; the launch traced here: 53.5 us
  Pallas kernels  52.1 us (97%)
  local copies, waits for them, and re-layouts  1.4 us (3%)
    pallas_call x1, Pallas kernels, local(): pl.pallas_call(kernel, out_shape=jax.ShapeDtypeStruct((ROWS, D), BF16), i...  52.1 us
    unnamed x1, local copies, waits for them, and re-layouts  1.4 us

profile of v7, /device:TPU:1, one launch (start us, length us, event | category | flops | bytes accessed | tf_op | source)
XLA Modules:
  0.0 53.5 jit_solution(5578128196954215281)
XLA Ops:
  0.0 52.1 %layer.1 = bf16[16,1280]{1,0:T(8,128)(2,1)} custom-call(bf16[16,1280]{1,0:T(8,128)(2,1)} %frames.1, f32[1280]{0:T(1024)} %ln_gain.1, bf16[1280,256]{1,0:T(8,128)(2,1)} %w_query.1, bf16[1024,256]{1,0:T(8,128)(2,1)} %keys.1, bf16[1024,256]{1,0:T(8,128)(2,1)} %values.1, s32[4,256]{1,0:T(4,128)} %active.1, bf16[256,1280]{1,0:T(8,128)(2,1)} %w_out.1, ...), custom_call_target="tpu_custom_call" | custom-call | tf_op jit(solution)/shard_map/layer/pallas_call | solution.py:387
  52.1 1.4 %copy.12 = bf16[16,1280]{1,0:T(8,128)(2,1)} copy(bf16[16,1280]{1,0:T(8,128)(2,1)} %layer.1) | data formatting | bytes 81920

commit v8 on v7

--- a/solution.py
+++ b/solution.py
@@ -36,7 +36,7 @@
     fr, lng, ffg, wq, kb, vb, act, wo, wu, wd,
     qown, qb, pb, po, ry, zs, rz, ty, tr, ts, tz, cx, rs, yo, xr, rc, bias, wb, upper,
     ld, s_kv, r_kv, s_fr, r_fr, s_q, r_q, r_up, s_fw, s_yf, r_yf, s_ry, r_ry, s_rz, r_rz,
-    s_ty, r_ty, s_tz, r_tz, s_xf, r_xf, s_xa, r_xa, s_xr, r_xr, s_rc, r_rc,
+    s_ty, r_ty, s_tz, r_tz, s_xf, r_xf, s_xa, r_xa, s_xr, r_xr, s_rc, r_rc, turn,
 ):
     x = lax.axis_index("dp")
     b = lax.axis_index("bank")
@@ -197,14 +197,6 @@
             forward(k, e).start()
     sent += [forward(k, e) for k in range(4) for e in (1, 2, 3)]
 
-    frames_out = [send(fr.at[0], fr.at[NX - e], s_xf.at[e - 1], r_xf.at[NX - e - 1], dev(dx=e)) for e in (2, 1, 3)]
-    sent1 += frames_out
-
-    @pl.when(c == 1)
-    def _():
-        for copy in frames_out:
-            copy.start()
-
     for n in range(4, 6):
         loads[n].wait()
     arrived(kb.at[1 - c], r_kv.at[0])
@@ -256,7 +248,6 @@
             copy.start()
 
     def attend(k, carry):
-        pl.when((k == 3) & (c == 0))(lambda: add_up(0))
         for e in (1, 3, 2):
             arrived(qb.at[k, e], r_yf.at[k, e - 1])
         q = qb[k].reshape(STEP, BIAS)
@@ -275,7 +266,7 @@
         po[k] = num[:part]
         for e in (2, 1, 3):
             pb[k, e - 1] = num[e * part : (e + 1) * part].astype(BF16)
-            give_back(k, e).start()
+            pl.when(c == 1)(give_back(k, e).start)
         row = lax.dot_general(
             jnp.ones((8, 128), BF16), tot.astype(BF16), (((1,), (1,)), ((), ())), preferred_element_type=F32
         )
@@ -294,9 +285,21 @@
 
     for copy in totals_back[1]:
         copy.start()
+
+    @pl.when(c == 1)
+    def _():
+        pl.semaphore_signal(turn, inc=1, device_id=sibling, device_id_type=MESH)
+
+    @pl.when(c == 0)
+    def _():
+        pl.semaphore_wait(turn, 1)
+        for k in range(4):
+            for e in (2, 1, 3):
+                give_back(k, e).start()
+
     sent += totals_back[0] + totals_back[1]
 
-    pl.when(c == 1)(lambda: add_up(0))
+    add_up(0)
     add_up(1)
     add_up(2)
     add_totals(0)
@@ -304,6 +307,14 @@
     add_totals(1)
     sent += totals_out
     sent += [to_owner(k, j) for k in range(4) for j in (0, 1)]
+
+    frames_out = [send(fr.at[0], fr.at[NX - e], s_xf.at[e - 1], r_xf.at[NX - e - 1], dev(dx=e)) for e in (2, 1, 3)]
+    sent1 += frames_out
+
+    @pl.when(c == 1)
+    def _():
+        for copy in frames_out:
+            copy.start()
 
     for n in range(6, 10):
         loads[n].wait()
@@ -432,6 +443,7 @@
             dma((3,)), dma((3,)),
             dma((2, 8)), dma((2, 4)),
             dma, dma,
+            pltpu.SemaphoreType.REGULAR,
         ],
         compiler_params=pltpu.CompilerParams(
             collective_id=0, has_side_effects=True, vmem_limit_bytes=56 * 2**20

time: 53.7 us -> 52.2 us (0.972)
  Pallas kernels: 52.1 us -> 50.6 us
    pallas_call x1, Pallas kernels: 52.1 us -> 50.6 us  [local(): pl.pallas_call(kernel, out_shape=jax.ShapeDtypeStruct((ROWS, D), BF16), i...]
where the time goes in v8:
time: 52.2 us; the launch traced here: 52 us
  Pallas kernels  50.6 us (97%)
  local copies, waits for them, and re-layouts  1.4 us (3%)
    pallas_call x1, Pallas kernels, local(): pl.pallas_call(kernel, out_shape=jax.ShapeDtypeStruct((ROWS, D), BF16), i...  50.6 us
    unnamed x1, local copies, waits for them, and re-layouts  1.4 us

profile of v8, /device:TPU:1, one launch (start us, length us, event | category | flops | bytes accessed | tf_op | source)
XLA Modules:
  0.0 52.0 jit_solution(1627729097864825722)
XLA Ops:
  0.0 50.6 %layer.1 = bf16[16,1280]{1,0:T(8,128)(2,1)} custom-call(bf16[16,1280]{1,0:T(8,128)(2,1)} %frames.1, f32[1280]{0:T(1024)} %ln_gain.1, bf16[1280,256]{1,0:T(8,128)(2,1)} %w_query.1, bf16[1024,256]{1,0:T(8,128)(2,1)} %keys.1, bf16[1024,256]{1,0:T(8,128)(2,1)} %values.1, s32[4,256]{1,0:T(4,128)} %active.1, bf16[256,1280]{1,0:T(8,128)(2,1)} %w_out.1, ...), custom_call_target="tpu_custom_call" | custom-call | tf_op jit(solution)/shard_map/layer/pallas_call | solution.py:398
  50.6 1.4 %copy.12 = bf16[16,1280]{1,0:T(8,128)(2,1)} copy(bf16[16,1280]{1,0:T(8,128)(2,1)} %layer.1) | data formatting | bytes 81920

commit v9 on v8

--- a/solution.py
+++ b/solution.py
@@ -128,7 +128,7 @@
         send(qown, upper, s_q.at[9], r_up, dev(dz=-4, core=1)),
         send(qown, slot(0), s_q.at[8], r_q.at[0], dev(dz=4, core=1)),
     ] + [
-        send(qown, slot(i), s_q.at[i], r_q.at[i], dev(dz=-NEAR[i], core=0)) for i in range(7, -1, -1)
+        send(qown, slot(i), s_q.at[i], r_q.at[i], dev(dz=-NEAR[i], core=0)) for i in range(8)
     ]
     relay_down = [
         send(upper, slot(2 * n - 1), s_fw.at[2 * n - 1], r_q.at[2 * n - 1], dev(dz=-n, core=1)) for n in (4, 3, 2, 1)

time: 52.2 us -> 51.4 us (0.985)
  Pallas kernels: 50.6 us -> 49.8 us
    pallas_call x1, Pallas kernels: 50.6 us -> 49.8 us  [local(): pl.pallas_call(kernel, out_shape=jax.ShapeDtypeStruct((ROWS, D), BF16), i...]
where the time goes in v9:
time: 51.4 us; the launch traced here: 51.2 us
  Pallas kernels  49.8 us (97%)
  local copies, waits for them, and re-layouts  1.4 us (3%)
    pallas_call x1, Pallas kernels, local(): pl.pallas_call(kernel, out_shape=jax.ShapeDtypeStruct((ROWS, D), BF16), i...  49.8 us
    unnamed x1, local copies, waits for them, and re-layouts  1.4 us

profile of v9, /device:TPU:1, one launch (start us, length us, event | category | flops | bytes accessed | tf_op | source)
XLA Modules:
  0.0 51.2 jit_solution(6106306896682850123)
XLA Ops:
  0.0 49.8 %layer.1 = bf16[16,1280]{1,0:T(8,128)(2,1)} custom-call(bf16[16,1280]{1,0:T(8,128)(2,1)} %frames.1, f32[1280]{0:T(1024)} %ln_gain.1, bf16[1280,256]{1,0:T(8,128)(2,1)} %w_query.1, bf16[1024,256]{1,0:T(8,128)(2,1)} %keys.1, bf16[1024,256]{1,0:T(8,128)(2,1)} %values.1, s32[4,256]{1,0:T(4,128)} %active.1, bf16[256,1280]{1,0:T(8,128)(2,1)} %w_out.1, ...), custom_call_target="tpu_custom_call" | custom-call | tf_op jit(solution)/shard_map/layer/pallas_call | solution.py:398
  49.8 1.4 %copy.12 = bf16[16,1280]{1,0:T(8,128)(2,1)} copy(bf16[16,1280]{1,0:T(8,128)(2,1)} %layer.1) | data formatting | bytes 81920

commit v10 on v9

--- a/solution.py
+++ b/solution.py
@@ -131,9 +131,9 @@
         send(qown, slot(i), s_q.at[i], r_q.at[i], dev(dz=-NEAR[i], core=0)) for i in range(8)
     ]
     relay_down = [
-        send(upper, slot(2 * n - 1), s_fw.at[2 * n - 1], r_q.at[2 * n - 1], dev(dz=-n, core=1)) for n in (4, 3, 2, 1)
-    ]
-    relay_up = [send(slot(0), slot(2 * n), s_fw.at[2 * n], r_q.at[2 * n], dev(dz=n, core=1)) for n in (3, 2, 1)]
+        send(upper, slot(2 * n - 1), s_fw.at[2 * n - 1], r_q.at[2 * n - 1], dev(dz=-n, core=1)) for n in (1, 2, 3, 4)
+    ]
+    relay_up = [send(slot(0), slot(2 * n), s_fw.at[2 * n], r_q.at[2 * n], dev(dz=n, core=1)) for n in (1, 2, 3)]
 
     def forward(k, e):
         return send(qb.at[k, 0], qb.at[k, NY - e], s_yf.at[k, e - 1], r_yf.at[k, NY - e - 1], dev(dy=e))

time: 51.4 us -> 50.6 us (0.984)
  Pallas kernels: 49.8 us -> 49.1 us
    pallas_call x1, Pallas kernels: 49.8 us -> 49.1 us  [local(): pl.pallas_call(kernel, out_shape=jax.ShapeDtypeStruct((ROWS, D), BF16), i...]
where the time goes in v10:
time: 50.6 us; the launch traced here: 50.5 us
  Pallas kernels  49.1 us (97%)
  local copies, waits for them, and re-layouts  1.4 us (3%)
    pallas_call x1, Pallas kernels, local(): pl.pallas_call(kernel, out_shape=jax.ShapeDtypeStruct((ROWS, D), BF16), i...  49.1 us
    unnamed x1, local copies, waits for them, and re-layouts  1.4 us

profile of v10, /device:TPU:1, one launch (start us, length us, event | category | flops | bytes accessed | tf_op | source)
XLA Modules:
  0.0 50.5 jit_solution(12681236598809662745)
XLA Ops:
  0.0 49.1 %layer.1 = bf16[16,1280]{1,0:T(8,128)(2,1)} custom-call(bf16[16,1280]{1,0:T(8,128)(2,1)} %frames.1, f32[1280]{0:T(1024)} %ln_gain.1, bf16[1280,256]{1,0:T(8,128)(2,1)} %w_query.1, bf16[1024,256]{1,0:T(8,128)(2,1)} %keys.1, bf16[1024,256]{1,0:T(8,128)(2,1)} %values.1, s32[4,256]{1,0:T(4,128)} %active.1, bf16[256,1280]{1,0:T(8,128)(2,1)} %w_out.1, ...), custom_call_target="tpu_custom_call" | custom-call | tf_op jit(solution)/shard_map/layer/pallas_call | solution.py:398
  49.1 1.4 %copy.12 = bf16[16,1280]{1,0:T(8,128)(2,1)} copy(bf16[16,1280]{1,0:T(8,128)(2,1)} %layer.1) | data formatting | bytes 81920

commit v11 on v10

--- a/solution.py
+++ b/solution.py
@@ -165,8 +165,10 @@
         for copy in query_out:
             copy.start()
 
-    keys_over.start()
-    values_over.start()
+    @pl.when(c == 0)
+    def _():
+        keys_over.start()
+        values_over.start()
 
     loads[3].wait()
     first = (z * NY + y) * 16
@@ -188,6 +190,8 @@
     def _():
         for copy in relay_up:
             copy.start()
+        keys_over.start()
+        values_over.start()
 
     for k in range(4):
         for i in (2 * k, 2 * k + 1):

time: 50.6 us -> 50.6 us (level)
  no operation moved by 1% of the time
where the time goes in v11:
time: 50.6 us; the launch traced here: 50.5 us
  Pallas kernels  49.1 us (97%)
  local copies, waits for them, and re-layouts  1.4 us (3%)
    pallas_call x1, Pallas kernels, local(): pl.pallas_call(kernel, out_shape=jax.ShapeDtypeStruct((ROWS, D), BF16), i...  49.1 us
    unnamed x1, local copies, waits for them, and re-layouts  1.4 us

profile of v11, /device:TPU:1, one launch (start us, length us, event | category | flops | bytes accessed | tf_op | source)
XLA Modules:
  0.0 50.5 jit_solution(10774864525483762953)
XLA Ops:
  0.0 49.1 %layer.1 = bf16[16,1280]{1,0:T(8,128)(2,1)} custom-call(bf16[16,1280]{1,0:T(8,128)(2,1)} %frames.1, f32[1280]{0:T(1024)} %ln_gain.1, bf16[1280,256]{1,0:T(8,128)(2,1)} %w_query.1, bf16[1024,256]{1,0:T(8,128)(2,1)} %keys.1, bf16[1024,256]{1,0:T(8,128)(2,1)} %values.1, s32[4,256]{1,0:T(4,128)} %active.1, bf16[256,1280]{1,0:T(8,128)(2,1)} %w_out.1, ...), custom_call_target="tpu_custom_call" | custom-call | tf_op jit(solution)/shard_map/layer/pallas_call | solution.py:402
  49.1 1.4 %copy.12 = bf16[16,1280]{1,0:T(8,128)(2,1)} copy(bf16[16,1280]{1,0:T(8,128)(2,1)} %layer.1) | data formatting | bytes 81920
